TPU v7x, 512 devices: a whole 4x8x8 slice. The times are simulated.
512 devices in a mesh: wide: 64 (over z, x, core), grp: 8 (over y).
Axes of the slice: x: 4, y: 8, z: 8, core: 2. Of those that a mesh axis runs over, the one named last changes fastest.
Arguments:
- amplitudes: float32 [256, 128, 128], P('wide'), may hold values from -6 to 6
- integrals: float32 [256, 128, 128], P('wide'), may hold values from -0.046875 to 0.046875
- residual_in: float32 [256, 128, 128], P('wide'), may hold values from -6 to 6
- task_lists: int32 [64, 8, 128, 3], P('wide', 'grp'), may hold values from 0 to 63
- task_counts: int32 [64, 8], P('wide'), may hold values from 1 to 128, 576 in all within a row
- amp_wanted: int32 [64, 64], P('wide'), may hold values from 0 to 3
- int_wanted: int32 [64, 64], P('wide'), may hold values from 0 to 3
- res_targets: int32 [64, 64], P('wide'), may hold values from 0 to 3
Outputs:
- residual_out: float32 [256, 128, 128], P('wide')
Inputs may be any that keep to these rules, and one draw needn't show every extreme that they name: `task_counts`: the counts of one group's 8 members add up to 576; in every group one member has exactly 128.
All inputs are finite; a program needn't handle non-finite values.
Results may differ from a plain program's by a relative error of at most 0.0003.
Values sent between devices are 32-bit elements; how exact they have to be, the bound alone decides.
No kernel may reach another device: no remote copies, remote signals or barrier semaphores. Data moves between devices by JAX's collectives and lax.ppermute only.
A program may use at most 64 MiB of HBM per device.

v0:
```python
import jax
import jax.numpy as jnp
from jax import lax
from jax.sharding import PartitionSpec as P


def accumulate(tiles_a, tiles_b, chosen, valid_mask, wide_count, live_total):
    tile_size = tiles_a.shape[1]
    block_len = 16
    length = chosen.shape[0]
    padding = -length % block_len
    chosen = jnp.concatenate([chosen, jnp.zeros((padding, 3), jnp.int32)], axis=0)
    valid_mask = jnp.concatenate([valid_mask, jnp.zeros((padding,), jnp.float32)], axis=0)
    block_total = (live_total + block_len - 1) // block_len

    def one_block(index, running):
        block_tasks = lax.dynamic_slice_in_dim(chosen, index * block_len, block_len, 0)
        block_live = lax.dynamic_slice_in_dim(valid_mask, index * block_len, block_len, 0)
        left = tiles_a[block_tasks[:, 0]]
        right = tiles_b[block_tasks[:, 1]]
        products = jnp.einsum(
            "kab,kcb->kac",
            left,
            right,
            precision=lax.Precision.HIGHEST,
            preferred_element_type=jnp.float32,
        )
        products = products * block_live[:, None, None]
        return running.at[block_tasks[:, 2]].add(products)

    start_acc = jnp.zeros((wide_count, tile_size, tile_size), jnp.float32)
    return lax.fori_loop(0, block_total, one_block, start_acc)


def local(
    amplitudes, integrals, residual_in, task_lists, task_counts, amp_wanted, int_wanted, res_targets
):
    wide_count = lax.axis_size("wide")
    group_count = lax.axis_size("grp")
    member = lax.axis_index("grp")
    tile_size = amplitudes.shape[1]
    per_device = task_lists.shape[2]
    row_count = tile_size // group_count
    requests = jnp.stack([amp_wanted[0], int_wanted[0], res_targets[0]], axis=1)
    asked_for = lax.all_to_all(requests, "wide", split_axis=0, concat_axis=0, tiled=True)
    served_a = amplitudes[asked_for[:, 0]]
    served_b = integrals[asked_for[:, 1]]
    tiles_a, tiles_b = (
        lax.all_to_all(served_a, "wide", split_axis=0, concat_axis=0, tiled=True),
        lax.all_to_all(served_b, "wide", split_axis=0, concat_axis=0, tiled=True),
    )
    slot_ids = jnp.arange(per_device, dtype=jnp.int32)
    chosen = task_lists[0, 0]
    valid_mask = (slot_ids < task_counts[0][member]).astype(jnp.float32)
    running = accumulate(tiles_a, tiles_b, chosen, valid_mask, wide_count, chosen.shape[0])
    partial_value = lax.psum_scatter(running, "grp", scatter_dimension=1, tiled=True)
    returned = lax.all_to_all(partial_value, "wide", split_axis=0, concat_axis=0, tiled=True)
    rows_here = lax.dynamic_slice_in_dim(residual_in, member * row_count, row_count, 1)
    rows_here = rows_here.at[asked_for[:, 2]].add(returned)
    return lax.all_gather(rows_here, "grp", axis=1, tiled=True)


def solution(mesh):
    placed = (
        P("wide", None, None),
        P("wide", None, None),
        P("wide", None, None),
        P("wide", "grp", None, None),
        P("wide", None),
        P("wide", None),
        P("wide", None),
        P("wide", None),
    )
    return jax.shard_map(
        local, mesh=mesh, in_specs=placed, out_specs=P("wide", None, None), check_vma=False
    )
```

profile of v0, /device:TPU:1, one launch (start us, length us, event | category | flops | bytes accessed | tf_op | source)
XLA Modules:
  0.0 444.4 jit_solution(12874216385700648113)
XLA Ops:
  6.5 0.7 add_bitcast_fusion
  7.4 24.0 %all_to_all.27 = s32[64,1,3]{2,1,0:T(1,128)S(1)} all-to-all(s32[64,1,3]{2,1,0:T(1,128)S(1)} %copy.10), channel_id=1, replica_groups=mesh['wide'=64,'grp'=8] {'wide'}, dimensions={0} | all-to-all | bytes 1536 | tf_op jit(solution)/shard_map/all_to_all | solution.py:45
  31.6 2.8 gather_fusion.2
  34.4 5.8 %all-to-all-start.1 = ((f32[64,128,128]{2,1,0:T(8,128)}), f32[64,128,128]{2,1,0:T(8,128)}, u32[]{:S(2)}, u32[]{:S(2)}) async-start(f32[64,128,128]{2,1,0:T(8,128)} %gather_fusion.2), calls=%async_computation.1 | async-start | bytes 8388608 | tf_op jit(solution)/shard_map/all_to_all | solution.py:49
  40.3 2.8 gather_fusion.3
  43.1 91.8 %all-to-all-done.1 = f32[64,128,128]{2,1,0:T(8,128)} async-done(((f32[64,128,128]{2,1,0:T(8,128)}), f32[64,128,128]{2,1,0:T(8,128)}, u32[]{:S(2)}, u32[]{:S(2)}) %all-to-all-start.1) | async-done | bytes 4194336 | tf_op jit(solution)/shard_map/all_to_all | solution.py:49
  134.9 7.2 %all-to-all-start.2 = ((f32[64,128,128]{2,1,0:T(8,128)}), f32[64,128,128]{2,1,0:T(8,128)}, u32[]{:S(2)}, u32[]{:S(2)}) async-start(f32[64,128,128]{2,1,0:T(8,128)} %gather_fusion.3), calls=%async_computation.2 | async-start | bytes 8388608 | tf_op jit(solution)/shard_map/all_to_all | solution.py:50
  143.5 93.4 %all-to-all-done.2 = f32[64,128,128]{2,1,0:T(8,128)} async-done(((f32[64,128,128]{2,1,0:T(8,128)}), f32[64,128,128]{2,1,0:T(8,128)}, u32[]{:S(2)}, u32[]{:S(2)}) %all-to-all-start.2) | async-done | bytes 4194336 | tf_op jit(solution)/shard_map/all_to_all | solution.py:50
  236.8 2.5 broadcast_in_dim.18
  239.3 91.6 %while.13 = (s32[]{:T(128)}, f32[64,128,128]{2,1,0:T(8,128)}, s32[128,3]{0,1:T(4,128)S(1)}, f32[64,128,128]{2,1,0:T(8,128)}, f32[64,128,128]{2,1,0:T(8,128)}, /*...) while((s32[]{:T(128)}, f32[64,128,128]{2,1,0:T(8,128)}, s32[128,3]{0,1:T(4,128)S(1)}, ...), condition=%wide.region_2.0_spmd, body=%wide.region_0.0_spmd.sunk | while | flops 403179680 | bytes 10495387 | solution.py:32
  239.5 2.8 gather_fusion
  242.3 2.8 gather_fusion.1
  245.1 2.3 convolution_multiply_fusion.2
  247.4 3.4 scatter_fusion
  250.9 2.8 gather_fusion
  253.7 2.8 gather_fusion.1
  256.5 2.3 convolution_multiply_fusion.2
  258.8 3.4 scatter_fusion
  262.4 2.8 gather_fusion
  265.2 2.8 gather_fusion.1
  268.0 2.3 convolution_multiply_fusion.2
  270.3 3.4 scatter_fusion
  273.8 2.8 gather_fusion
  276.6 2.8 gather_fusion.1
  279.4 2.3 convolution_multiply_fusion.2
  281.7 3.4 scatter_fusion
  285.3 2.8 gather_fusion
  288.1 2.8 gather_fusion.1
  290.9 2.3 convolution_multiply_fusion.2
  293.2 3.4 scatter_fusion
  296.8 2.8 gather_fusion
  299.6 2.8 gather_fusion.1
  302.4 2.3 convolution_multiply_fusion.2
  304.7 3.4 scatter_fusion
  308.2 2.8 gather_fusion
  311.1 2.8 gather_fusion.1
  313.9 2.3 convolution_multiply_fusion.2
  316.2 3.3 scatter_fusion
  319.6 2.8 gather_fusion
  322.5 2.8 gather_fusion.1
  325.3 2.3 convolution_multiply_fusion.2
  327.6 3.4 scatter_fusion
  331.0 55.5 %reduce-scatter.2.cloned.1.call-done = f32[64,16,128]{2,1,0:T(8,128)} async-done(((f32[64,128,128]{2,1,0:T(8,128)}), f32[64,16,128]{2,1,0:T(8,128)}) %reduce-scatter.2.cloned.1.call-update) | async-done | bytes 524304 | tf_op jit(solution)/shard_map/reduce_scatter | solution.py:56
  386.4 11.0 %all-to-all-start.3 = ((f32[64,16,128]{2,1,0:T(8,128)}), f32[64,16,128]{2,1,0:T(8,128)S(1)}, u32[]{:S(2)}, u32[]{:S(2)}) async-start(f32[64,16,128]{2,1,0:T(8,128)} %reduce-scatter.2.cloned.1.call-done), calls=%async_computation.4 | async-start | bytes 1048576 | tf_op jit(solution)/shard_map/all_to_all | solution.py:57
  397.4 0.8 constant_dynamic-slice_fusion.2
  398.2 16.9 %all-to-all-done.3 = f32[64,16,128]{2,1,0:T(8,128)S(1)} async-done(((f32[64,16,128]{2,1,0:T(8,128)}), f32[64,16,128]{2,1,0:T(8,128)S(1)}, u32[]{:S(2)}, u32[]{:S(2)}) %all-to-all-start.3) | async-done | bytes 524320 | tf_op jit(solution)/shard_map/all_to_all | solution.py:57
  415.1 3.0 scatter_fusion.1
  418.1 18.8 %all_gather.3 = f32[4,128,128]{2,1,0:T(8,128)S(1)} all-gather(f32[4,16,128]{2,1,0:T(8,128)S(1)} %scatter_fusion.1), channel_id=1, replica_groups=mesh['wide'=64,'grp'=8] {'grp'}, dimensions={1}, use_global_device_ids=true | all-gather | bytes 294912 | tf_op jit(solution)/shard_map/all_gather | solution.py:60
  (50 shorter events, 3.6 us)
Async XLA Ops:
  6.5 25.1 %copy-start = (f32[4,128,128]{2,1,0:T(8,128)S(1)}, f32[4,128,128]{2,1,0:T(8,128)}, u32[]{:S(2)}) copy-start(f32[4,128,128]{2,1,0:T(8,128)} %param.10) | copy-start | bytes 786436
  34.4 5.9 %copy-start.1 = (f32[4,128,128]{2,1,0:T(8,128)S(1)}, f32[4,128,128]{2,1,0:T(8,128)}, u32[]{:S(2)}) copy-start(f32[4,128,128]{2,1,0:T(8,128)} %param.11) | copy-start | bytes 786436
  34.4 100.5 %all-to-all-start.1 = ((f32[64,128,128]{2,1,0:T(8,128)}), f32[64,128,128]{2,1,0:T(8,128)}, u32[]{:S(2)}, u32[]{:S(2)}) async-start(f32[64,128,128]{2,1,0:T(8,128)} %gather_fusion.2), calls=%async_computation.1 | async-start | bytes 8388608 | tf_op jit(solution)/shard_map/all_to_all | solution.py:49
  43.1 99.2 %copy-start.2 = (s32[1,1,128,3]{2,1,3,0:T(1,128)S(1)}, s32[1,1,128,3]{2,1,3,0:T(1,128)}, u32[]{:S(2)}) copy-start(s32[1,1,128,3]{2,1,3,0:T(1,128)} %param.13) | copy-start | bytes 4612
  43.1 99.2 %copy-start.3 = (s32[1,8]{1,0:T(1,128)S(1)}, s32[1,8]{1,0:T(1,128)}, u32[]{:S(2)}) copy-start(s32[1,8]{1,0:T(1,128)} %param.14) | copy-start | bytes 100
  134.9 101.9 %all-to-all-start.2 = ((f32[64,128,128]{2,1,0:T(8,128)}), f32[64,128,128]{2,1,0:T(8,128)}, u32[]{:S(2)}, u32[]{:S(2)}) async-start(f32[64,128,128]{2,1,0:T(8,128)} %gather_fusion.3), calls=%async_computation.2 | async-start | bytes 8388608 | tf_op jit(solution)/shard_map/all_to_all | solution.py:50
  142.2 244.3 %reduce-scatter.2.cloned.1.call-start = ((), (), s32[]{:S(2)}) async-start(), calls=%async_computation.5 | async-start | bytes 4718592 | tf_op jit(solution)/shard_map/reduce_scatter | solution.py:56
  386.4 28.7 %all-to-all-start.3 = ((f32[64,16,128]{2,1,0:T(8,128)}), f32[64,16,128]{2,1,0:T(8,128)S(1)}, u32[]{:S(2)}, u32[]{:S(2)}) async-start(f32[64,16,128]{2,1,0:T(8,128)} %reduce-scatter.2.cloned.1.call-done), calls=%async_computation.4 | async-start | bytes 1048576 | tf_op jit(solution)/shard_map/all_to_all | solution.py:57
Sparse Core Ops, SparseCore 0:
  331.1 55.2 reduce-scatter.1
where the time goes:
time: 451 us; the launch traced here: 444 us
  waiting for transfers between devices  258 us (57%)
  local copies, waits for them, and re-layouts  56.2 us (12%)
  blocking collectives  42.8 us (9%)
  other arithmetic  31.7 us (7%)
  starting transfers between devices  24.1 us (5%)
  matrix products  18.3 us (4%)
  between operations  13.5 us (3%)
    all_to_all x1, waiting for transfers between devices, local(): lax.all_to_all(served_b, 'wide', split_axis=0, concat_axis=0, tiled=True)  93.4 us
    all_to_all x1, waiting for transfers between devices, local(): lax.all_to_all(served_a, 'wide', split_axis=0, concat_axis=0, tiled=True)  91.8 us
    reduce_scatter x1, waiting for transfers between devices, local(): lax.psum_scatter(running, 'grp', scatter_dimension=1, tiled=True)  55.5 us
    scatter-add x8, other arithmetic, one_block(): return running.at[block_tasks[:, 2]].add(products)  27 us
    all_to_all x1, blocking collectives, local(): lax.all_to_all(requests, 'wide', split_axis=0, concat_axis=0, tiled=True)  24 us
    gather x8, local copies, waits for them, and re-layouts, one_block(): right = tiles_b[block_tasks[:, 1]]  22.4 us
    gather x8, local copies, waits for them, and re-layouts, one_block(): left = tiles_a[block_tasks[:, 0]]  22.4 us
    all_gather x1, blocking collectives, local(): return lax.all_gather(rows_here, 'grp', axis=1, tiled=True)  18.8 us
  transfers between devices with their start and end apart: 4, of which 4 were waited for; matrix products, arithmetic and copies ran while one was open for 1% of the time, Pallas kernels for 0%

commit v1 on v0

v1 whole, which is shorter than its diff:
```python
import jax
import jax.numpy as jnp
from jax import lax
from jax.experimental import pallas as pl
from jax.experimental.pallas import tpu as pltpu
from jax.sharding import Mesh, PartitionSpec as P

TB = 128
TILES = 4
OWNERS = 64
MEMBERS = 8
KS = TB // MEMBERS
ALL_TILES = OWNERS * TILES
ROWS = 2 * TILES * KS + 3 * MEMBERS
A_AT, B_AT, T_AT = 0, TILES * KS, 2 * TILES * KS
LISTS = OWNERS * MEMBERS
CHUNK = 256
SUB = 32

NT = (((1,), (1,)), ((), ()))
TN = (((0,), (0,)), ((), ()))


def dot(a, b, dims=(((1,), (0,)), ((), ()))):
    return lax.dot_general(a, b, dims, preferred_element_type=jnp.float32)


def task_kernel(tasks_ref, counts_ref, amp_ref, int_ref, res_ref, out_ref):
    live = counts_ref[0, lax.axis_index("grp")]
    slot = lax.broadcasted_iota(jnp.int32, (TB, OWNERS), 0)
    owner = lax.broadcasted_iota(jnp.int32, (TB, OWNERS), 1)
    number = lax.broadcasted_iota(jnp.int32, (8, OWNERS), 1) * TILES
    rows = []
    for column, table in enumerate((amp_ref, int_ref, res_ref)):
        hit = tasks_ref[:, column : column + 1] == owner
        if column == 2:
            hit = hit & (slot < live)
        names = number + table[0:1, :] + (1 if column == 2 else 0)
        rows.append(dot(names.astype(jnp.bfloat16), hit.astype(jnp.bfloat16), NT)[0:1])
    rows[2] = rows[2] - 1.0
    block = jnp.concatenate(rows + [jnp.zeros((5, TB), jnp.float32)], axis=0)
    for member in range(MEMBERS):
        out_ref[member] = block


def payload_kernel(amp_ref, int_ref, tasks_ref, out_ref, turned):
    first = pl.multiple_of(lax.axis_index("grp") * KS, KS)
    for at, tiles in ((A_AT, amp_ref), (B_AT, int_ref)):
        for t in range(TILES):
            turned[...] = tiles[t].T
            rows = turned[pl.ds(first, KS), :]
            for z in range(8):
                out_ref[z, at + t * KS : at + (t + 1) * KS, :] = rows
    for kind in range(3):
        rows = jnp.concatenate([tasks_ref[m, kind : kind + 1, :] for m in range(MEMBERS)], axis=0)
        for z in range(8):
            out_ref[z, T_AT + kind * MEMBERS : T_AT + (kind + 1) * MEMBERS, :] = rows


def ladder_kernel(own_ref, other_ref, out_ref, sa, sb, lhs, rhs, acc, wanted, names, lists_v, lists_s, sem):
    me = ((lax.axis_index("z") * 4) + lax.axis_index("x")) * 2 + lax.axis_index("core")
    core = lax.axis_index("core")

    def spread(index, _):
        x, z = index // 8, index % 8
        for side, ref, c in ((0, own_ref, core), (1, other_ref, 1 - core)):
            owner = (z * 4 + x) * 2 + c
            to = pl.ds(pl.multiple_of(owner * TILES * KS, TILES * KS), TILES * KS)
            for at, store in ((A_AT, sa), (B_AT, sb)):
                value = ref[x, z, at : at + TILES * KS, :]
                high = value.astype(jnp.bfloat16)
                store[to, 0:TB] = high
                store[to, TB : 2 * TB] = (value - high.astype(jnp.float32)).astype(jnp.bfloat16)
        return 0

    lax.fori_loop(0, 32, spread, 0)
    sa[ALL_TILES * KS :, :] = jnp.zeros((KS, 2 * TB), jnp.bfloat16)
    acc[...] = jnp.zeros_like(acc)

    for side, ref in enumerate((own_ref, other_ref)):
        for x in range(4):
            for z in range(0, 8, 2):
                at = (side * 32 + x * 8 + z) * MEMBERS
                for kind in range(3):
                    rows = [ref[x, z + i, T_AT + kind * MEMBERS : T_AT + (kind + 1) * MEMBERS, :] for i in range(2)]
                    rows = jnp.concatenate(rows, axis=0)
                    if kind == 2:
                        wanted[at : at + 2 * MEMBERS, :] = rows
                    else:
                        names[at : at + 2 * MEMBERS, kind * TB : (kind + 1) * TB] = rows.astype(jnp.bfloat16)

    upto = lax.broadcasted_iota(jnp.int32, (TB, TB), 0) <= lax.broadcasted_iota(jnp.int32, (TB, TB), 1)
    upto = upto.astype(jnp.bfloat16)
    ones = jnp.ones((8, TB), jnp.bfloat16)

    def one_round(state):
        turn, _ = state
        base = turn * CHUNK
        for t in range(TILES):
            hit = wanted[...] == (me * TILES + t).astype(jnp.float32)
            hit_f = hit.astype(jnp.float32)
            hit_b = hit_f.astype(jnp.bfloat16)
            place = dot(hit_b, upto)
            names[:, 2 * TB :] = (place * hit_f).astype(jnp.bfloat16)
            totals = dot(ones, hit_b, NT)
            carry = jnp.zeros((8, 1), jnp.float32)
            upper = []
            for i in range(LISTS // TB):
                piece = totals[:, i * TB : (i + 1) * TB]
                upper.append(dot(piece.astype(jnp.bfloat16), upto) + carry)
                carry = carry + jnp.sum(piece, axis=1, keepdims=True)
            upper = jnp.concatenate(upper, axis=1)
            lower = upper - totals
            rank = (base + lax.broadcasted_iota(jnp.int32, (CHUNK, LISTS), 0)).astype(jnp.float32)
            row = (lower[0:1] <= rank) & (rank < upper[0:1])
            before = jnp.sum(jnp.where(row, lower[0:1], 0.0), axis=1, keepdims=True)
            found = dot(row.astype(jnp.float32).astype(jnp.bfloat16), names[...])
            pick = found[:, 2 * TB :] == rank[:, 0:1] + 1.0 - before
            left = dot(ones, jnp.where(pick, found[:, 0:TB], 0.0).astype(jnp.bfloat16), NT)
            right = dot(ones, jnp.where(pick, found[:, TB : 2 * TB], 0.0).astype(jnp.bfloat16), NT)
            entry = (base + lax.broadcasted_iota(jnp.int32, (8, CHUNK), 1)).astype(jnp.float32)
            code = jnp.where(entry < carry, left * 256.0 + right, float(ALL_TILES * 256))
            lists_v[t : t + 1, :] = code[0:1].astype(jnp.int32)
            lists_v[TILES + t : TILES + t + 1, :] = jnp.broadcast_to(carry[0:1], (1, CHUNK)).astype(jnp.int32)
        copy = pltpu.make_async_copy(lists_v, lists_s, sem)
        copy.start()
        copy.wait()
        most = jnp.int32(0)
        for t in range(TILES):
            total = lists_s[TILES + t, 0]
            most = jnp.maximum(most, total)
            here = jnp.clip(total - base, 0, CHUNK)

            def block(index, _, t=t):
                for i in range(SUB):
                    code = lists_s[t, index * SUB + i]
                    a = pl.multiple_of((code >> 8) * KS, KS)
                    b = pl.multiple_of((code & 255) * KS, KS)
                    lhs[i * KS : (i + 1) * KS, :] = sa[pl.ds(a, KS), :]
                    rhs[i * KS : (i + 1) * KS, :] = sb[pl.ds(b, KS), :]
                acc[t] += dot(lhs[...], rhs[...], TN)
                return 0

            lax.fori_loop(0, (here + SUB - 1) // SUB, block, 0)
        return turn + 1, (most + CHUNK - 1) // CHUNK

    lax.while_loop(lambda s: s[0] < s[1], one_round, (jnp.int32(0), jnp.int32(1)))
    for t in range(TILES):
        total = (acc[t, 0:TB, 0:TB] + acc[t, 0:TB, TB:]) + (acc[t, TB:, 0:TB] + acc[t, TB:, TB:])
        for m in range(MEMBERS):
            out_ref[m, t] = total[m * KS : (m + 1) * KS, :]


VMEM = pl.BlockSpec(memory_space=pltpu.VMEM)
SMEM = pl.BlockSpec(memory_space=pltpu.SMEM)
PARAMS = pltpu.CompilerParams(vmem_limit_bytes=48 * 1024 * 1024)


def swap(block, axis):
    return lax.all_to_all(block, axis, split_axis=0, concat_axis=0, tiled=True)


def local(amplitudes, integrals, residual_in, task_lists, task_counts, amp_wanted, int_wanted, res_targets):
    f32 = jnp.float32
    tasks = pl.pallas_call(
        task_kernel,
        out_shape=jax.ShapeDtypeStruct((MEMBERS, 8, TB), f32),
        in_specs=[VMEM, SMEM, VMEM, VMEM, VMEM],
        out_specs=VMEM,
    )(task_lists[0, 0], task_counts, amp_wanted, int_wanted, res_targets)
    tasks = swap(tasks, "grp")
    payload = pl.pallas_call(
        payload_kernel,
        out_shape=jax.ShapeDtypeStruct((8, ROWS, TB), f32),
        in_specs=[VMEM] * 3,
        out_specs=VMEM,
        scratch_shapes=[pltpu.VMEM((TB, TB), f32)],
    )(amplitudes, integrals, tasks)
    along_z = swap(payload, "z")
    own = swap(jnp.broadcast_to(along_z[None], (4, 8, ROWS, TB)), "x")
    other = lax.ppermute(own, "core", [(0, 1), (1, 0)])
    bf16 = jnp.bfloat16
    partial = pl.pallas_call(
        ladder_kernel,
        out_shape=jax.ShapeDtypeStruct((MEMBERS, TILES, KS, TB), f32),
        in_specs=[VMEM, VMEM],
        out_specs=VMEM,
        scratch_shapes=[
            pltpu.VMEM(((ALL_TILES + 1) * KS, 2 * TB), bf16),
            pltpu.VMEM((ALL_TILES * KS, 2 * TB), bf16),
            pltpu.VMEM((SUB * KS, 2 * TB), bf16),
            pltpu.VMEM((SUB * KS, 2 * TB), bf16),
            pltpu.VMEM((TILES, 2 * TB, 2 * TB), f32),
            pltpu.VMEM((LISTS, TB), f32),
            pltpu.VMEM((LISTS, 3 * TB), bf16),
            pltpu.VMEM((2 * TILES, CHUNK), jnp.int32),
            pltpu.SMEM((2 * TILES, CHUNK), jnp.int32),
            pltpu.SemaphoreType.DMA,
        ],
        compiler_params=PARAMS,
    )(own, other)
    member = lax.axis_index("grp")
    rows = lax.dynamic_slice_in_dim(residual_in, member * KS, KS, 1)
    rows = rows + jnp.sum(swap(partial, "grp"), axis=0)
    whole = swap(jnp.broadcast_to(rows[None], (MEMBERS, TILES, KS, TB)), "grp")
    return whole.transpose(1, 0, 2, 3).reshape(TILES, TB, TB)


def solution(mesh):
    fine = Mesh(mesh.devices.reshape(8, 4, 2, MEMBERS), ("z", "x", "core", "grp"))
    wide = ("z", "x", "core")
    placed = (
        P(wide, None, None),
        P(wide, None, None),
        P(wide, None, None),
        P(wide, "grp", None, None),
        P(wide, None),
        P(wide, None),
        P(wide, None),
        P(wide, None),
    )
    return jax.shard_map(local, mesh=fine, in_specs=placed, out_specs=P(wide, None, None), check_vma=False)
```

time: 451 us -> 132 us (0.29); the launches traced: 444 us -> 132 us
  waiting for transfers between devices: 258 us -> 16.6 us
  local copies, waits for them, and re-layouts: 56.2 us -> 2.32 us
  blocking collectives: 42.8 us -> 85.5 us
  other arithmetic: 31.7 us -> 0.8 us
  matrix products: 18.3 us -> 0 us
  Pallas kernels: 0 us -> 15.6 us
  between operations: 13.5 us -> 0.05 us
  starting transfers between devices: 24.1 us -> 10.7 us
    all_to_all x3 -> x1, waiting for transfers between devices: 202 us -> 12.3 us  [swap(): return lax.all_to_all(block, axis, split_axis=0, concat_axis=0, tiled=True)]
    all_to_all x1 -> x4, blocking collectives: 24 us -> 85.5 us  [swap(): return lax.all_to_all(block, axis, split_axis=0, concat_axis=0, tiled=True)]
    reduce_scatter x1 -> x0, waiting for transfers between devices: 55.5 us -> none  [local(): lax.psum_scatter(running, 'grp', scatter_dimension=1, tiled=True)]
    gather x18 -> x0, local copies, waits for them, and re-layouts: 50.4 us -> none  [the longest x8 22.4 us: one_block(): right = tiles_b[block_tasks[:, 1]]]
    scatter-add x9 -> x0, other arithmetic: 30 us -> none  [the longest x8 27 us: one_block(): return running.at[block_tasks[:, 2]].add(products)]
    all_to_all x3 -> x1, starting transfers between devices: 24 us -> 3.42 us  [swap(): return lax.all_to_all(block, axis, split_axis=0, concat_axis=0, tiled=True)]
    all_gather x1 -> x0, blocking collectives: 18.8 us -> none  [local(): return lax.all_gather(rows_here, 'grp', axis=1, tiled=True)]
    dot_general x8 -> x0, matrix products: 18.3 us -> none  [one_block(): jnp.einsum('kab,kcb->kac', left, right, precision=lax.Precision.HIGHEST,...]
  transfers between devices with their start and end apart: 4 -> 2, of which waited for: 4 -> 2; matrix products, arithmetic and copies ran while one was open for 1% -> 0% of each run, Pallas kernels for 0% -> 0%
where the time goes in v1:
time: 132 us
  blocking collectives  85.5 us (65%)
  waiting for transfers between devices  16.6 us (13%)
  Pallas kernels  15.6 us (12%)
  starting transfers between devices  10.7 us (8%)
  local copies, waits for them, and re-layouts  2.32 us (2%)
    all_to_all x4, blocking collectives, swap(): return lax.all_to_all(block, axis, split_axis=0, concat_axis=0, tiled=True)  85.5 us
    all_to_all x1, waiting for transfers between devices, swap(): return lax.all_to_all(block, axis, split_axis=0, concat_axis=0, tiled=True)  12.3 us
    pallas_call x1, Pallas kernels, local(): pl.pallas_call(ladder_kernel, out_shape=jax.ShapeDtypeStruct((MEMBERS, TI...  11.7 us
    ppermute x1, starting transfers between devices, local(): other = lax.ppermute(own, 'core', [(0, 1), (1, 0)])  7.32 us
    ppermute x1, waiting for transfers between devices, local(): other = lax.ppermute(own, 'core', [(0, 1), (1, 0)])  4.33 us
    all_to_all x1, starting transfers between devices, swap(): return lax.all_to_all(block, axis, split_axis=0, concat_axis=0, tiled=True)  3.42 us
  transfers between devices with their start and end apart: 2, of which 2 were waited for; matrix products, arithmetic and copies ran while one was open for 0% of the time, Pallas kernels for 0%

profile of v1, /device:TPU:1, one launch (start us, length us, event | category | flops | bytes accessed | tf_op | source)
XLA Modules:
  0.0 131.6 jit_solution(7645411774541958160)
XLA Ops:
  0.0 1.4 %copy.11 = s32[1,1,128,3]{3,2,1,0:T(8,128)} copy(s32[1,1,128,3]{2,1,3,0:T(1,128)} %param.11) | data formatting | bytes 3072 | tf_op args[3]
  1.4 1.7 %shard_map.82 = f32[8,8,128]{2,1,0:T(8,128)} custom-call(s32[128,3]{1,0:T(8,128)} %bitcast.4, s32[1,8]{1,0:T(1,128)} %counts_ref.1, s32[1,64]{1,0:T(1,128)} %amp_ref.2, s32[1,64]{1,0:T(1,128)} %int_ref.2, s32[1,64]{1,0:T(1,128)} %res_ref.1), custom_call_target="tpu_custom_call" | custom-call | tf_op jit(solution)/shard_map/pallas_call | solution.py:165
  3.2 14.6 %all_to_all.25.tasks_ref = f32[8,8,128]{2,1,0:T(8,128)} all-to-all(f32[8,8,128]{2,1,0:T(8,128)} %shard_map.82), channel_id=1, replica_groups=mesh['z'=8,'x'=4,'core'=2,'grp'=8] {'grp'}, dimensions={0} | all-to-all | bytes 65536 | tf_op jit(solution)/shard_map/all_to_all | solution.py:160
  17.8 2.1 %shard_map.83 = f32[8,152,128]{2,1,0:T(8,128)} custom-call(f32[4,128,128]{2,1,0:T(8,128)} %amp_ref.3, f32[4,128,128]{2,1,0:T(8,128)} %int_ref.3, f32[8,8,128]{2,1,0:T(8,128)} %all_to_all.25.tasks_ref), custom_call_target="tpu_custom_call" | custom-call | tf_op jit(solution)/shard_map/pallas_call | solution.py:172
  19.9 26.4 %all_to_all.26 = f32[8,152,128]{2,1,0:T(8,128)S(1)} all-to-all(f32[8,152,128]{2,1,0:T(8,128)} %shard_map.83), channel_id=1, replica_groups=mesh['z'=8,'x'=4,'core'=2,'grp'=8] {'z'}, dimensions={0} | all-to-all | bytes 1245184 | tf_op jit(solution)/shard_map/all_to_all | solution.py:160
  46.2 0.2 broadcast_in_dim.4
  46.4 29.9 %all_to_all.27.own_ref = f32[4,8,152,128]{3,2,1,0:T(8,128)S(1)} all-to-all(f32[4,8,152,128]{3,2,1,0:T(8,128)S(1)} %broadcast_in_dim.4), channel_id=1, replica_groups=mesh['z'=8,'x'=4,'core'=2,'grp'=8] {'x'}, dimensions={0} | all-to-all | bytes 4980736 | tf_op jit(solution)/shard_map/all_to_all | solution.py:160
  76.3 7.3 %collective-permute-start = (f32[4,8,152,128]{3,2,1,0:T(8,128)S(1)}, f32[4,8,152,128]{3,2,1,0:T(8,128)S(1)}, u32[]{:S(2)}, u32[]{:S(2)}) collective-permute-start(f32[4,8,152,128]{3,2,1,0:T(8,128)S(1)} %all_to_all.27.own_ref), channel_id=1, source_target_pairs={{0,8},{8,0},{1,9},{9,1},{2,10},{10,2},{3,11},{11,3},{4,12},{12,4},... | collective-permute-start | bytes 7471112 | tf_op jit(solution)/shard_map/ppermute | solution.py:181
  83.6 4.3 %collective-permute-done.other_ref = f32[4,8,152,128]{3,2,1,0:T(8,128)S(1)} collective-permute-done((f32[4,8,152,128]{3,2,1,0:T(8,128)S(1)}, f32[4,8,152,128]{3,2,1,0:T(8,128)S(1)}, u32[]{:S(2)}, u32[]{:S(2)}) %collective-permute-start) | collective-permute-done | bytes 2490400 | tf_op jit(solution)/shard_map/ppermute | solution.py:181
  87.9 11.7 %shard_map.84 = f32[8,4,16,128]{3,2,1,0:T(8,128)} custom-call(f32[4,8,152,128]{3,2,1,0:T(8,128)S(1)} %all_to_all.27.own_ref, f32[4,8,152,128]{3,2,1,0:T(8,128)S(1)} %collective-permute-done.other_ref), custom_call_target="tpu_custom_call" | custom-call | tf_op jit(solution)/shard_map/pallas_call | solution.py:183
  99.7 3.4 %all-to-all-start.3 = ((f32[8,4,16,128]{3,2,1,0:T(8,128)}), f32[8,4,16,128]{3,2,1,0:T(8,128)S(1)}, u32[]{:S(2)}, u32[]{:S(2)}) async-start(f32[8,4,16,128]{3,2,1,0:T(8,128)} %shard_map.84), calls=%async_computation.3 | async-start | bytes 524288 | tf_op jit(solution)/shard_map/all_to_all | solution.py:160
  103.1 12.3 %all-to-all-done.3 = f32[8,4,16,128]{3,2,1,0:T(8,128)S(1)} async-done(((f32[8,4,16,128]{3,2,1,0:T(8,128)}), f32[8,4,16,128]{3,2,1,0:T(8,128)S(1)}, u32[]{:S(2)}, u32[]{:S(2)}) %all-to-all-start.3) | async-done | bytes 262176 | tf_op jit(solution)/shard_map/all_to_all | solution.py:160
  115.4 0.8 dynamic-slice_add_fusion
  116.2 14.6 %all_to_all.28 = f32[8,4,16,128]{3,2,1,0:T(8,128)S(1)} all-to-all(f32[8,4,16,128]{3,2,1,0:T(8,128)S(1)} %broadcast_in_dim.5), channel_id=1, replica_groups=mesh['z'=8,'x'=4,'core'=2,'grp'=8] {'grp'}, dimensions={0} | all-to-all | bytes 524288 | tf_op jit(solution)/shard_map/all_to_all | solution.py:160
  130.9 0.7 copy.12
  (2 shorter events, 0.0 us)
Async XLA Ops:
  76.3 11.7 %collective-permute-start = (f32[4,8,152,128]{3,2,1,0:T(8,128)S(1)}, f32[4,8,152,128]{3,2,1,0:T(8,128)S(1)}, u32[]{:S(2)}, u32[]{:S(2)}) collective-permute-start(f32[4,8,152,128]{3,2,1,0:T(8,128)S(1)} %all_to_all.27.own_ref), channel_id=1, source_target_pairs={{0,8},{8,0},{1,9},{9,1},{2,10},{10,2},{3,11},{11,3},{4,12},{12,4},... | collective-permute-start | bytes 7471112 | tf_op jit(solution)/shard_map/ppermute | solution.py:181
  99.7 15.7 %all-to-all-start.3 = ((f32[8,4,16,128]{3,2,1,0:T(8,128)}), f32[8,4,16,128]{3,2,1,0:T(8,128)S(1)}, u32[]{:S(2)}, u32[]{:S(2)}) async-start(f32[8,4,16,128]{3,2,1,0:T(8,128)} %shard_map.84), calls=%async_computation.3 | async-start | bytes 524288 | tf_op jit(solution)/shard_map/all_to_all | solution.py:160

commit v2 on v1

v2 whole, which is shorter than its diff:
```python
import jax
import jax.numpy as jnp
from jax import lax
from jax.experimental import pallas as pl
from jax.experimental.pallas import tpu as pltpu
from jax.sharding import Mesh, PartitionSpec as P

TB = 128
TILES = 4
OWNERS = 64
MEMBERS = 8
KS = TB // MEMBERS
ALL_TILES = OWNERS * TILES
ROWS = 2 * TILES * KS + 3 * MEMBERS
A_AT, B_AT, T_AT = 0, TILES * KS, 2 * TILES * KS
LISTS = OWNERS * MEMBERS
CHUNK = 256
SUB = 32

NT = (((1,), (1,)), ((), ()))
TN = (((0,), (0,)), ((), ()))


def dot(a, b, dims=(((1,), (0,)), ((), ()))):
    return lax.dot_general(a, b, dims, preferred_element_type=jnp.float32)


def task_kernel(tasks_ref, counts_ref, amp_ref, int_ref, res_ref, out_ref):
    live = counts_ref[0, lax.axis_index("grp")]
    owner = lax.broadcasted_iota(jnp.int32, (OWNERS, TB), 0)
    slot = lax.broadcasted_iota(jnp.int32, (OWNERS, TB), 1)
    number = lax.broadcasted_iota(jnp.int32, (8, OWNERS), 1) * TILES
    for kind, table in enumerate((amp_ref, int_ref, res_ref)):
        hit = tasks_ref[0, kind] == owner
        if kind == 2:
            hit = hit & (slot < live)
        names = number + table[0:1, :] + (1 if kind == 2 else 0)
        row = dot(names.astype(jnp.bfloat16), hit.astype(jnp.bfloat16))[0:1]
        row = row - 1.0 if kind == 2 else row
        for m in range(MEMBERS):
            out_ref[m, kind : kind + 1, :] = row


def turn_kernel(amp_ref, int_ref, out_ref, turned):
    first = pl.multiple_of(lax.axis_index("grp") * KS, KS)
    for at, tiles in ((A_AT, amp_ref), (B_AT, int_ref)):
        for t in range(TILES):
            turned[t] = tiles[t].T
        for t in range(TILES):
            out_ref[at + t * KS : at + (t + 1) * KS, :] = turned[t, pl.ds(first, KS), :]


def payload_kernel(tiles_ref, lists_ref, out_ref):
    for kind in range(3):
        rows = jnp.concatenate([lists_ref[m, kind : kind + 1, :] for m in range(MEMBERS)], axis=0)
        for z in range(8):
            out_ref[z, T_AT + kind * MEMBERS : T_AT + (kind + 1) * MEMBERS, :] = rows
    for z in range(8):
        out_ref[z, 0:T_AT, :] = tiles_ref[...]


def ladder_kernel(*refs):
    out_ref, sa, sb, lhs, rhs, acc, wanted, names, lists_v, lists_s, sem = refs[10:]
    my_x = lax.axis_index("x")
    blocks = [(ref, side, *(((0, 0, 8), (3, 0, 8), (1, 0, 8), (2, 0, 4), (2, 4, 4))[i])) for side in range(2) for i, ref in enumerate(refs[side * 5 : side * 5 + 5])]
    me = ((lax.axis_index("z") * 4) + lax.axis_index("x")) * 2 + lax.axis_index("core")
    core = lax.axis_index("core")

    at = 0
    for ref, _, _, _, size in blocks:
        for z in range(0, size, 2):
            for kind in range(3):
                rows = [ref[z + i, T_AT + kind * MEMBERS : T_AT + (kind + 1) * MEMBERS, :] for i in range(2)]
                rows = jnp.concatenate(rows, axis=0)
                if kind == 2:
                    wanted[at : at + 2 * MEMBERS, :] = rows
                else:
                    names[at : at + 2 * MEMBERS, kind * TB : (kind + 1) * TB] = rows.astype(jnp.bfloat16)
            at += 2 * MEMBERS

    upto = lax.broadcasted_iota(jnp.int32, (TB, TB), 0) <= lax.broadcasted_iota(jnp.int32, (TB, TB), 1)
    upto = upto.astype(jnp.bfloat16)
    ones = jnp.ones((8, TB), jnp.bfloat16)

    def pick(base):
        hits = []
        for t in range(TILES):
            hit = wanted[...] == (me * TILES + t).astype(jnp.float32)
            hits.append(hit.astype(jnp.float32).astype(jnp.bfloat16))
        totals = [dot(ones, hit, NT) for hit in hits]
        for t in range(TILES):
            place = dot(hits[t], upto)
            names[:, (2 + t) * TB : (3 + t) * TB] = place.astype(jnp.bfloat16) * hits[t]
        lowers, uppers, sums = [], [], []
        for t in range(TILES):
            carry = jnp.zeros((8, 1), jnp.float32)
            upper = []
            pieces = [totals[t][:, i * TB : (i + 1) * TB] for i in range(LISTS // TB)]
            within = [dot(piece.astype(jnp.bfloat16), upto) for piece in pieces]
            for i in range(LISTS // TB):
                upper.append(within[i] + carry)
                carry = carry + within[i][:, TB - 1 : TB]
            uppers.append(jnp.concatenate(upper, axis=1))
            lowers.append(uppers[t] - totals[t])
            sums.append(carry)
        rank = (base + lax.broadcasted_iota(jnp.int32, (CHUNK, LISTS), 0)).astype(jnp.float32)
        entry = (base + lax.broadcasted_iota(jnp.int32, (8, CHUNK), 1)).astype(jnp.float32)
        rows = [(lowers[t][0:1] <= rank) & (rank < uppers[t][0:1]) for t in range(TILES)]
        before = [jnp.sum(jnp.where(rows[t], lowers[t][0:1], 0.0), axis=1, keepdims=True) for t in range(TILES)]
        rows = [row.astype(jnp.float32).astype(jnp.bfloat16) for row in rows]
        found = [dot(rows[t], names[:, 0 : 2 * TB]) for t in range(TILES)]
        places = [dot(rows[t], names[:, (2 + t) * TB : (3 + t) * TB]) for t in range(TILES)]
        for t in range(TILES):
            chosen = places[t] == rank[:, 0:1] + 1.0 - before[t]
            left = dot(ones, jnp.where(chosen, found[t][:, 0:TB], 0.0).astype(jnp.bfloat16), NT)
            right = dot(ones, jnp.where(chosen, found[t][:, TB : 2 * TB], 0.0).astype(jnp.bfloat16), NT)
            code = jnp.where(entry < sums[t], left * 256.0 + right, float(ALL_TILES * 256))
            lists_v[t : t + 1, :] = code[0:1].astype(jnp.int32)
            lists_v[TILES + t : TILES + t + 1, :] = jnp.broadcast_to(sums[t][0:1], (1, CHUNK)).astype(jnp.int32)

    def spread(index, _):
        for ref, side, step, first, size in blocks:
            if size == 4:
                ref = ref.at[pl.ds(index // 2, 1)]
            else:
                ref = ref.at[pl.ds(index, 1)]
            z = index // 2 + first if size == 4 else index
            c = core if side == 0 else 1 - core
            owner = (z * 4 + (my_x + step) % 4) * 2 + c
            to = pl.ds(pl.multiple_of(owner * TILES * KS, TILES * KS), TILES * KS)
            for at, store in ((A_AT, sa), (B_AT, sb)):
                value = ref[0, at : at + TILES * KS, :]
                high = value.astype(jnp.bfloat16)
                store[to, 0:TB] = high
                store[to, TB : 2 * TB] = (value - high.astype(jnp.float32)).astype(jnp.bfloat16)
        return 0

    def one_round(state):
        turn, _ = state
        base = turn * CHUNK
        pick(base)
        copy = pltpu.make_async_copy(lists_v, lists_s, sem)
        copy.start()

        @pl.when(turn == 0)
        def _():
            lax.fori_loop(0, 8, spread, 0)
            sa[ALL_TILES * KS :, :] = jnp.zeros((KS, 2 * TB), jnp.bfloat16)
            acc[...] = jnp.zeros_like(acc)

        copy.wait()
        most = lists_s[TILES, 0]
        for t in range(1, TILES):
            most = jnp.maximum(most, lists_s[TILES + t, 0])

        def block(index, _):
            for t in range(TILES):
                for i in range(SUB):
                    code = lists_s[t, index * SUB + i]
                    a = pl.multiple_of((code >> 8) * KS, KS)
                    b = pl.multiple_of((code & 255) * KS, KS)
                    lhs[t, i * KS : (i + 1) * KS, :] = sa[pl.ds(a, KS), :]
                    rhs[t, i * KS : (i + 1) * KS, :] = sb[pl.ds(b, KS), :]
            for t in range(TILES):
                acc[t] += dot(lhs[t], rhs[t], TN)
            return 0

        lax.fori_loop(0, (jnp.clip(most - base, 0, CHUNK) + SUB - 1) // SUB, block, 0)
        return turn + 1, (most + CHUNK - 1) // CHUNK

    lax.while_loop(lambda s: s[0] < s[1], one_round, (jnp.int32(0), jnp.int32(1)))
    for t in range(TILES):
        total = (acc[t, 0:TB, 0:TB] + acc[t, 0:TB, TB:]) + (acc[t, TB:, 0:TB] + acc[t, TB:, TB:])
        for m in range(MEMBERS):
            out_ref[m, t] = total[m * KS : (m + 1) * KS, :]


VMEM = pl.BlockSpec(memory_space=pltpu.VMEM)
SMEM = pl.BlockSpec(memory_space=pltpu.SMEM)
PARAMS = pltpu.CompilerParams(vmem_limit_bytes=48 * 1024 * 1024)


def shift(block, by):
    return lax.ppermute(block, "x", [(i, (i + by) % 4) for i in range(4)])


def swap(block, axis):
    return lax.all_to_all(block, axis, split_axis=0, concat_axis=0, tiled=True)


def local(amplitudes, integrals, residual_in, task_lists, task_counts, amp_wanted, int_wanted, res_targets):
    f32 = jnp.float32
    lists = pl.pallas_call(
        task_kernel,
        out_shape=jax.ShapeDtypeStruct((MEMBERS, 3, TB), f32),
        in_specs=[VMEM, SMEM, VMEM, VMEM, VMEM],
        out_specs=VMEM,
    )(task_lists.transpose(0, 3, 1, 2), task_counts, amp_wanted, int_wanted, res_targets)
    lists = swap(lists, "grp")
    tiles = pl.pallas_call(
        turn_kernel,
        out_shape=jax.ShapeDtypeStruct((T_AT, TB), f32),
        in_specs=[VMEM] * 2,
        out_specs=VMEM,
        scratch_shapes=[pltpu.VMEM((TILES, TB, TB), f32)],
    )(amplitudes, integrals)
    payload = pl.pallas_call(
        payload_kernel,
        out_shape=jax.ShapeDtypeStruct((8, ROWS, TB), f32),
        in_specs=[VMEM] * 2,
        out_specs=VMEM,
    )(tiles, lists)
    here = swap(payload, "z")
    left, right = shift(here, 1), shift(here, -1)
    near = [here, left, right, shift(left[:4], 1), shift(right[4:], -1)]
    far = [lax.ppermute(block, "core", [(0, 1), (1, 0)]) for block in near]
    bf16 = jnp.bfloat16
    partial = pl.pallas_call(
        ladder_kernel,
        out_shape=jax.ShapeDtypeStruct((MEMBERS, TILES, KS, TB), f32),
        in_specs=[VMEM] * 10,
        out_specs=VMEM,
        scratch_shapes=[
            pltpu.VMEM(((ALL_TILES + 1) * KS, 2 * TB), bf16),
            pltpu.VMEM((ALL_TILES * KS, 2 * TB), bf16),
            pltpu.VMEM((TILES, SUB * KS, 2 * TB), bf16),
            pltpu.VMEM((TILES, SUB * KS, 2 * TB), bf16),
            pltpu.VMEM((TILES, 2 * TB, 2 * TB), f32),
            pltpu.VMEM((LISTS, TB), f32),
            pltpu.VMEM((LISTS, (2 + TILES) * TB), bf16),
            pltpu.VMEM((2 * TILES, CHUNK), jnp.int32),
            pltpu.SMEM((2 * TILES, CHUNK), jnp.int32),
            pltpu.SemaphoreType.DMA,
        ],
        compiler_params=PARAMS,
    )(*near, *far)
    member = lax.axis_index("grp")
    rows = lax.dynamic_slice_in_dim(residual_in, member * KS, KS, 1)
    rows = rows + jnp.sum(swap(partial, "grp"), axis=0)
    whole = swap(jnp.broadcast_to(rows[None], (MEMBERS, TILES, KS, TB)), "grp")
    return whole.transpose(1, 0, 2, 3).reshape(TILES, TB, TB)


def solution(mesh):
    fine = Mesh(mesh.devices.reshape(8, 4, 2, MEMBERS), ("z", "x", "core", "grp"))
    wide = ("z", "x", "core")
    placed = (
        P(wide, None, None),
        P(wide, None, None),
        P(wide, None, None),
        P(wide, "grp", None, None),
        P(wide, None),
        P(wide, None),
        P(wide, None),
        P(wide, None),
    )
    return jax.shard_map(local, mesh=fine, in_specs=placed, out_specs=P(wide, None, None), check_vma=False)
```

time: 132 us -> 123 us (0.932)
  blocking collectives: 85.5 us -> 41.1 us
  starting transfers between devices: 10.7 us -> 44.6 us
  waiting for transfers between devices: 16.6 us -> 19.7 us
    all_to_all x4 -> x2, blocking collectives: 85.5 us -> 41.1 us  [swap(): return lax.all_to_all(block, axis, split_axis=0, concat_axis=0, tiled=True)]
    ppermute x1 -> x9, starting transfers between devices: 7.32 us -> 33.5 us  [the longest x5 20.6 us: local(): far = [lax.ppermute(block, 'core', [(0, 1), (1, 0)]) for block in near]]
    all_to_all x1 -> x2, starting transfers between devices: 3.42 us -> 11.1 us  [swap(): return lax.all_to_all(block, axis, split_axis=0, concat_axis=0, tiled=True)]
    all_to_all x1 -> x2, waiting for transfers between devices: 12.3 us -> 16.9 us  [swap(): return lax.all_to_all(block, axis, split_axis=0, concat_axis=0, tiled=True)]
    pallas_call x1, Pallas kernels: 11.7 us -> 9.33 us  [local(): pl.pallas_call(ladder_kernel, out_shape=jax.ShapeDtypeStruct((MEMBERS, TI...]
    pallas_call x1 -> x2, Pallas kernels: 1.74 us -> 3.4 us  [the longest x1 1.86 us: local(): pl.pallas_call(turn_kernel, out_shape=jax.ShapeDtypeStruct((T_AT, TB), f3...]
    ppermute x1 -> x9, waiting for transfers between devices: 4.33 us -> 2.76 us  [the longest x5 1.56 us: local(): far = [lax.ppermute(block, 'core', [(0, 1), (1, 0)]) for block in near]]
  transfers between devices with their start and end apart: 2 -> 11, of which waited for: 2 -> 4; matrix products, arithmetic and copies ran while one was open for 0% -> 0% of each run, Pallas kernels for 0% -> 2%
where the time goes in v2:
time: 123 us; the launch traced here: 122 us
  starting transfers between devices  44.6 us (36%)
  blocking collectives  41.1 us (33%)
  waiting for transfers between devices  19.7 us (16%)
  Pallas kernels  14.4 us (12%)
  local copies, waits for them, and re-layouts  1.38 us (1%)
    all_to_all x2, blocking collectives, swap(): return lax.all_to_all(block, axis, split_axis=0, concat_axis=0, tiled=True)  41.1 us
    ppermute x5, starting transfers between devices, local(): far = [lax.ppermute(block, 'core', [(0, 1), (1, 0)]) for block in near]  20.6 us
    all_to_all x2, waiting for transfers between devices, swap(): return lax.all_to_all(block, axis, split_axis=0, concat_axis=0, tiled=True)  16.9 us
    ppermute x4, starting transfers between devices, shift(): return lax.ppermute(block, 'x', [(i, (i + by) % 4) for i in range(4)])  13 us
    all_to_all x2, starting transfers between devices, swap(): return lax.all_to_all(block, axis, split_axis=0, concat_axis=0, tiled=True)  11.1 us
    pallas_call x1, Pallas kernels, local(): pl.pallas_call(ladder_kernel, out_shape=jax.ShapeDtypeStruct((MEMBERS, TI...  9.33 us
  transfers between devices with their start and end apart: 11, of which 4 were waited for; matrix products, arithmetic and copies ran while one was open for 0% of the time, Pallas kernels for 2%

profile of v2, /device:TPU:1, one launch (start us, length us, event | category | flops | bytes accessed | tf_op | source)
XLA Modules:
  0.0 122.1 jit_solution(8634868543967461308)
XLA Ops:
  0.0 1.5 %shard_map.83 = f32[8,3,128]{2,1,0:T(4,128)} custom-call(s32[1,3,1,128]{3,2,1,0:T(1,128)} %bitcast.4, s32[1,8]{1,0:T(1,128)} %counts_ref.1, s32[1,64]{1,0:T(1,128)} %amp_ref.3, s32[1,64]{1,0:T(1,128)} %int_ref.3, s32[1,64]{1,0:T(1,128)} %res_ref.1), custom_call_target="tpu_custom_call" | custom-call | tf_op jit(solution)/shard_map/pallas_call | solution.py:193
  1.5 7.7 %all-to-all-start = ((f32[8,3,128]{2,1,0:T(4,128)}), f32[8,3,128]{2,1,0:T(4,128)S(1)}, u32[]{:S(2)}, u32[]{:S(2)}) async-start(f32[8,3,128]{2,1,0:T(4,128)} %shard_map.83), calls=%async_computation | async-start | bytes 32768 | tf_op jit(solution)/shard_map/all_to_all | solution.py:188
  9.2 1.9 %shard_map.82.tiles_ref = f32[128,128]{1,0:T(8,128)} custom-call(f32[4,128,128]{2,1,0:T(8,128)} %amp_ref.2, f32[4,128,128]{2,1,0:T(8,128)} %int_ref.2), custom_call_target="tpu_custom_call" | custom-call | tf_op jit(solution)/shard_map/pallas_call | solution.py:200
  11.1 4.8 %all-to-all-done.lists_ref = f32[8,3,128]{2,1,0:T(4,128)S(1)} async-done(((f32[8,3,128]{2,1,0:T(4,128)}), f32[8,3,128]{2,1,0:T(4,128)S(1)}, u32[]{:S(2)}, u32[]{:S(2)}) %all-to-all-start) | async-done | bytes 12320 | tf_op jit(solution)/shard_map/all_to_all | solution.py:188
  15.8 0.0 copy-start
  15.8 0.6 copy-done
  16.4 1.7 %shard_map.84 = f32[8,152,128]{2,1,0:T(8,128)} custom-call(f32[128,128]{1,0:T(8,128)} %shard_map.82.tiles_ref, f32[8,3,128]{2,1,0:T(4,128)} %copy-done), custom_call_target="tpu_custom_call" | custom-call | tf_op jit(solution)/shard_map/pallas_call | solution.py:207
  18.1 26.4 %all_to_all.20.refs_0_ = f32[8,152,128]{2,1,0:T(8,128)S(1)} all-to-all(f32[8,152,128]{2,1,0:T(8,128)} %shard_map.84), channel_id=1, replica_groups=mesh['z'=8,'x'=4,'core'=2,'grp'=8] {'z'}, dimensions={0} | all-to-all | bytes 1245184 | tf_op jit(solution)/shard_map/all_to_all | solution.py:188
  44.5 3.1 %collective-permute-start = (f32[8,152,128]{2,1,0:T(8,128)S(1)}, f32[8,152,128]{2,1,0:T(8,128)S(1)}, u32[]{:S(2)}, u32[]{:S(2)}) collective-permute-start(f32[8,152,128]{2,1,0:T(8,128)S(1)} %all_to_all.20.refs_0_), channel_id=1, source_target_pairs={{0,16},{16,32},{32,48},{48,0},{1,17},{17,33},{33,49},{49,1},{2,18}... | collective-permute-start | bytes 1867784 | tf_op jit(solution)/shard_map/ppermute | solution.py:184
  47.6 3.4 %collective-permute-start.1 = (f32[8,152,128]{2,1,0:T(8,128)S(1)}, f32[8,152,128]{2,1,0:T(8,128)S(1)}, u32[]{:S(2)}, u32[]{:S(2)}) collective-permute-start(f32[8,152,128]{2,1,0:T(8,128)S(1)} %all_to_all.20.refs_0_), channel_id=1, source_target_pairs={{0,48},{16,0},{32,16},{48,32},{1,49},{17,1},{33,17},{49,33},{2,50}... | collective-permute-start | bytes 1867784 | tf_op jit(solution)/shard_map/ppermute | solution.py:184
  51.0 6.7 %collective-permute-start.4 = (f32[8,152,128]{2,1,0:T(8,128)S(1)}, f32[8,152,128]{2,1,0:T(8,128)S(1)}, u32[]{:S(2)}, u32[]{:S(2)}) collective-permute-start(f32[8,152,128]{2,1,0:T(8,128)S(1)} %all_to_all.20.refs_0_), channel_id=1, source_target_pairs={{0,8},{8,0},{1,9},{9,1},{2,10},{10,2},{3,11},{11,3},{4,12},{12,4},... | collective-permute-start | bytes 1867784 | tf_op jit(solution)/shard_map/ppermute | solution.py:216
  57.7 1.2 collective-permute-done.refs_1_
  58.9 1.9 %collective-permute-start.2 = (f32[4,152,128]{2,1,0:T(8,128)S(1)}, f32[4,152,128]{2,1,0:T(8,128)S(1)}, u32[]{:S(2)}, u32[]{:S(2)}) collective-permute-start(f32[4,152,128]{2,1,0:T(8,128)S(1)} %slice.8), channel_id=1, source_target_pairs={{0,16},{16,32},{32,48},{48,0},{1,17},{17,33},{33,49},{49,1},{2,18}... | collective-permute-start | bytes 933896 | tf_op jit(solution)/shard_map/ppermute | solution.py:184
  60.8 0.0 collective-permute-done.1.refs_2_
  60.9 4.6 %collective-permute-start.3 = (f32[4,152,128]{2,1,0:T(8,128)S(1)}, f32[4,152,128]{2,1,0:T(8,128)S(1)}, u32[]{:S(2)}, u32[]{:S(2)}) collective-permute-start(f32[4,152,128]{2,1,0:T(8,128)S(1)} %slice.9), channel_id=1, source_target_pairs={{0,48},{16,0},{32,16},{48,32},{1,49},{17,1},{33,17},{49,33},{2,50}... | collective-permute-start | bytes 933896 | tf_op jit(solution)/shard_map/ppermute | solution.py:184
  65.5 7.6 %collective-permute-start.5 = (f32[8,152,128]{2,1,0:T(8,128)S(1)}, f32[8,152,128]{2,1,0:T(8,128)S(1)}, u32[]{:S(2)}, u32[]{:S(2)}) collective-permute-start(f32[8,152,128]{2,1,0:T(8,128)S(1)} %collective-permute-done.refs_1_), channel_id=1, source_target_pairs={{0,8},{8,0},{1,9},{9,1},{2,10},{10,2},{3,11},{11,3},{4,12},{12,4},... | collective-permute-start | bytes 1867784 | tf_op jit(solution)/shard_map/ppermute | solution.py:216
  73.1 1.9 %collective-permute-start.6 = (f32[8,152,128]{2,1,0:T(8,128)S(1)}, f32[8,152,128]{2,1,0:T(8,128)S(1)}, u32[]{:S(2)}, u32[]{:S(2)}) collective-permute-start(f32[8,152,128]{2,1,0:T(8,128)S(1)} %collective-permute-done.1.refs_2_), channel_id=1, source_target_pairs={{0,8},{8,0},{1,9},{9,1},{2,10},{10,2},{3,11},{11,3},{4,12},{12,4},... | collective-permute-start | bytes 1867784 | tf_op jit(solution)/shard_map/ppermute | solution.py:216
  75.0 0.0 collective-permute-done.2.refs_3_
  75.0 2.4 %collective-permute-start.7 = (f32[4,152,128]{2,1,0:T(8,128)S(1)}, f32[4,152,128]{2,1,0:T(8,128)S(1)}, u32[]{:S(2)}, u32[]{:S(2)}) collective-permute-start(f32[4,152,128]{2,1,0:T(8,128)S(1)} %collective-permute-done.2.refs_3_), channel_id=1, source_target_pairs={{0,8},{8,0},{1,9},{9,1},{2,10},{10,2},{3,11},{11,3},{4,12},{12,4},... | collective-permute-start | bytes 933896 | tf_op jit(solution)/shard_map/ppermute | solution.py:216
  77.4 0.0 collective-permute-done.3.refs_4_
  77.4 1.9 %collective-permute-start.8 = (f32[4,152,128]{2,1,0:T(8,128)S(1)}, f32[4,152,128]{2,1,0:T(8,128)S(1)}, u32[]{:S(2)}, u32[]{:S(2)}) collective-permute-start(f32[4,152,128]{2,1,0:T(8,128)S(1)} %collective-permute-done.3.refs_4_), channel_id=1, source_target_pairs={{0,8},{8,0},{1,9},{9,1},{2,10},{10,2},{3,11},{11,3},{4,12},{12,4},... | collective-permute-start | bytes 933896 | tf_op jit(solution)/shard_map/ppermute | solution.py:216
  79.4 0.0 collective-permute-done.4.refs_5_
  79.4 0.0 collective-permute-done.7.refs_8_
  79.4 1.6 %collective-permute-done.8.refs_9_ = f32[4,152,128]{2,1,0:T(8,128)S(1)} collective-permute-done((f32[4,152,128]{2,1,0:T(8,128)S(1)}, f32[4,152,128]{2,1,0:T(8,128)S(1)}, u32[]{:S(2)}, u32[]{:S(2)}) %collective-permute-start.8) | collective-permute-done | bytes 311328 | tf_op jit(solution)/shard_map/ppermute | solution.py:216
  80.9 0.0 collective-permute-done.5.refs_6_
  80.9 0.0 collective-permute-done.6.refs_7_
  80.9 9.3 %shard_map.85 = f32[8,4,16,128]{3,2,1,0:T(8,128)} custom-call(f32[8,152,128]{2,1,0:T(8,128)S(1)} %all_to_all.20.refs_0_, f32[8,152,128]{2,1,0:T(8,128)S(1)} %collective-permute-done.refs_1_, f32[8,152,128]{2,1,0:T(8,128)S(1)} %collective-permute-done.1.refs_2_, f32[4,152,128]{2,1,0:T(8,128)S(1)} %collective-permute-done.2.refs_3_, ...), custom_call_target="tpu_custom_call" | custom-call | tf_op jit(solution)/shard_map/pallas_call | solution.py:218
  90.3 3.4 %all-to-all-start.2 = ((f32[8,4,16,128]{3,2,1,0:T(8,128)}), f32[8,4,16,128]{3,2,1,0:T(8,128)S(1)}, u32[]{:S(2)}, u32[]{:S(2)}) async-start(f32[8,4,16,128]{3,2,1,0:T(8,128)} %shard_map.85), calls=%async_computation.2 | async-start | bytes 524288 | tf_op jit(solution)/shard_map/all_to_all | solution.py:188
  93.7 12.1 %all-to-all-done.2 = f32[8,4,16,128]{3,2,1,0:T(8,128)S(1)} async-done(((f32[8,4,16,128]{3,2,1,0:T(8,128)}), f32[8,4,16,128]{3,2,1,0:T(8,128)S(1)}, u32[]{:S(2)}, u32[]{:S(2)}) %all-to-all-start.2) | async-done | bytes 262176 | tf_op jit(solution)/shard_map/all_to_all | solution.py:188
  105.9 0.8 dynamic-slice_add_fusion
  106.7 14.7 %all_to_all.21 = f32[8,4,16,128]{3,2,1,0:T(8,128)S(1)} all-to-all(f32[8,4,16,128]{3,2,1,0:T(8,128)S(1)} %broadcast_in_dim.2), channel_id=1, replica_groups=mesh['z'=8,'x'=4,'core'=2,'grp'=8] {'grp'}, dimensions={0} | all-to-all | bytes 524288 | tf_op jit(solution)/shard_map/all_to_all | solution.py:188
  121.4 0.7 copy.9
  (4 shorter events, 0.1 us)
Async XLA Ops:
  1.5 14.3 %all-to-all-start = ((f32[8,3,128]{2,1,0:T(4,128)}), f32[8,3,128]{2,1,0:T(4,128)S(1)}, u32[]{:S(2)}, u32[]{:S(2)}) async-start(f32[8,3,128]{2,1,0:T(4,128)} %shard_map.83), calls=%async_computation | async-start | bytes 32768 | tf_op jit(solution)/shard_map/all_to_all | solution.py:188
  15.8 0.6 copy-start
  44.5 14.4 %collective-permute-start = (f32[8,152,128]{2,1,0:T(8,128)S(1)}, f32[8,152,128]{2,1,0:T(8,128)S(1)}, u32[]{:S(2)}, u32[]{:S(2)}) collective-permute-start(f32[8,152,128]{2,1,0:T(8,128)S(1)} %all_to_all.20.refs_0_), channel_id=1, source_target_pairs={{0,16},{16,32},{32,48},{48,0},{1,17},{17,33},{33,49},{49,1},{2,18}... | collective-permute-start | bytes 1867784 | tf_op jit(solution)/shard_map/ppermute | solution.py:184
  47.6 13.2 %collective-permute-start.1 = (f32[8,152,128]{2,1,0:T(8,128)S(1)}, f32[8,152,128]{2,1,0:T(8,128)S(1)}, u32[]{:S(2)}, u32[]{:S(2)}) collective-permute-start(f32[8,152,128]{2,1,0:T(8,128)S(1)} %all_to_all.20.refs_0_), channel_id=1, source_target_pairs={{0,48},{16,0},{32,16},{48,32},{1,49},{17,1},{33,17},{49,33},{2,50}... | collective-permute-start | bytes 1867784 | tf_op jit(solution)/shard_map/ppermute | solution.py:184
  51.0 28.4 %collective-permute-start.4 = (f32[8,152,128]{2,1,0:T(8,128)S(1)}, f32[8,152,128]{2,1,0:T(8,128)S(1)}, u32[]{:S(2)}, u32[]{:S(2)}) collective-permute-start(f32[8,152,128]{2,1,0:T(8,128)S(1)} %all_to_all.20.refs_0_), channel_id=1, source_target_pairs={{0,8},{8,0},{1,9},{9,1},{2,10},{10,2},{3,11},{11,3},{4,12},{12,4},... | collective-permute-start | bytes 1867784 | tf_op jit(solution)/shard_map/ppermute | solution.py:216
  58.9 16.1 %collective-permute-start.2 = (f32[4,152,128]{2,1,0:T(8,128)S(1)}, f32[4,152,128]{2,1,0:T(8,128)S(1)}, u32[]{:S(2)}, u32[]{:S(2)}) collective-permute-start(f32[4,152,128]{2,1,0:T(8,128)S(1)} %slice.8), channel_id=1, source_target_pairs={{0,16},{16,32},{32,48},{48,0},{1,17},{17,33},{33,49},{49,1},{2,18}... | collective-permute-start | bytes 933896 | tf_op jit(solution)/shard_map/ppermute | solution.py:184
  60.9 16.6 %collective-permute-start.3 = (f32[4,152,128]{2,1,0:T(8,128)S(1)}, f32[4,152,128]{2,1,0:T(8,128)S(1)}, u32[]{:S(2)}, u32[]{:S(2)}) collective-permute-start(f32[4,152,128]{2,1,0:T(8,128)S(1)} %slice.9), channel_id=1, source_target_pairs={{0,48},{16,0},{32,16},{48,32},{1,49},{17,1},{33,17},{49,33},{2,50}... | collective-permute-start | bytes 933896 | tf_op jit(solution)/shard_map/ppermute | solution.py:184
  65.5 15.5 %collective-permute-start.5 = (f32[8,152,128]{2,1,0:T(8,128)S(1)}, f32[8,152,128]{2,1,0:T(8,128)S(1)}, u32[]{:S(2)}, u32[]{:S(2)}) collective-permute-start(f32[8,152,128]{2,1,0:T(8,128)S(1)} %collective-permute-done.refs_1_), channel_id=1, source_target_pairs={{0,8},{8,0},{1,9},{9,1},{2,10},{10,2},{3,11},{11,3},{4,12},{12,4},... | collective-permute-start | bytes 1867784 | tf_op jit(solution)/shard_map/ppermute | solution.py:216
  73.1 7.9 %collective-permute-start.6 = (f32[8,152,128]{2,1,0:T(8,128)S(1)}, f32[8,152,128]{2,1,0:T(8,128)S(1)}, u32[]{:S(2)}, u32[]{:S(2)}) collective-permute-start(f32[8,152,128]{2,1,0:T(8,128)S(1)} %collective-permute-done.1.refs_2_), channel_id=1, source_target_pairs={{0,8},{8,0},{1,9},{9,1},{2,10},{10,2},{3,11},{11,3},{4,12},{12,4},... | collective-permute-start | bytes 1867784 | tf_op jit(solution)/shard_map/ppermute | solution.py:216
  75.0 4.4 %collective-permute-start.7 = (f32[4,152,128]{2,1,0:T(8,128)S(1)}, f32[4,152,128]{2,1,0:T(8,128)S(1)}, u32[]{:S(2)}, u32[]{:S(2)}) collective-permute-start(f32[4,152,128]{2,1,0:T(8,128)S(1)} %collective-permute-done.2.refs_3_), channel_id=1, source_target_pairs={{0,8},{8,0},{1,9},{9,1},{2,10},{10,2},{3,11},{11,3},{4,12},{12,4},... | collective-permute-start | bytes 933896 | tf_op jit(solution)/shard_map/ppermute | solution.py:216
  77.4 3.5 %collective-permute-start.8 = (f32[4,152,128]{2,1,0:T(8,128)S(1)}, f32[4,152,128]{2,1,0:T(8,128)S(1)}, u32[]{:S(2)}, u32[]{:S(2)}) collective-permute-start(f32[4,152,128]{2,1,0:T(8,128)S(1)} %collective-permute-done.3.refs_4_), channel_id=1, source_target_pairs={{0,8},{8,0},{1,9},{9,1},{2,10},{10,2},{3,11},{11,3},{4,12},{12,4},... | collective-permute-start | bytes 933896 | tf_op jit(solution)/shard_map/ppermute | solution.py:216
  90.3 15.6 %all-to-all-start.2 = ((f32[8,4,16,128]{3,2,1,0:T(8,128)}), f32[8,4,16,128]{3,2,1,0:T(8,128)S(1)}, u32[]{:S(2)}, u32[]{:S(2)}) async-start(f32[8,4,16,128]{3,2,1,0:T(8,128)} %shard_map.85), calls=%async_computation.2 | async-start | bytes 524288 | tf_op jit(solution)/shard_map/all_to_all | solution.py:188

commit v3 on v2

--- a/solution.py
+++ b/solution.py
@@ -11,11 +11,14 @@
 MEMBERS = 8
 KS = TB // MEMBERS
 ALL_TILES = OWNERS * TILES
-ROWS = 2 * TILES * KS + 3 * MEMBERS
+ROWS = 2 * TILES * KS + 16
+LIST_ROWS = 5
 A_AT, B_AT, T_AT = 0, TILES * KS, 2 * TILES * KS
-LISTS = OWNERS * MEMBERS
+LISTS = OWNERS * LIST_ROWS
 CHUNK = 256
 SUB = 32
+WAYS = 3
+WIDTH = CHUNK + 128
 
 NT = (((1,), (1,)), ((), ()))
 TN = (((0,), (0,)), ((), ()))
@@ -50,17 +53,25 @@
             out_ref[at + t * KS : at + (t + 1) * KS, :] = turned[t, pl.ds(first, KS), :]
 
 
-def payload_kernel(tiles_ref, lists_ref, out_ref):
-    for kind in range(3):
-        rows = jnp.concatenate([lists_ref[m, kind : kind + 1, :] for m in range(MEMBERS)], axis=0)
-        for z in range(8):
-            out_ref[z, T_AT + kind * MEMBERS : T_AT + (kind + 1) * MEMBERS, :] = rows
+def payload_kernel(counts_ref, tiles_ref, lists_ref, out_ref, joined):
+    joined[...] = jnp.full_like(joined, -1.0)
+    lane = lax.broadcasted_iota(jnp.int32, (3, TB), 1)
+    at = jnp.int32(0)
+    for m in range(MEMBERS):
+        row, by = at // TB, at % TB
+        turned = pltpu.roll(lists_ref[m], by, 1)
+        joined[row] = jnp.where(lane >= by, turned, joined[row])
+        joined[row + 1] = jnp.where(lane < by, turned, joined[row + 1])
+        at = at + counts_ref[0, m]
+    rows = [joined[i, kind : kind + 1, :] for kind in range(3) for i in range(LIST_ROWS)]
+    rows = jnp.concatenate(rows + [jnp.zeros((1, TB), jnp.float32)], axis=0)
     for z in range(8):
         out_ref[z, 0:T_AT, :] = tiles_ref[...]
+        out_ref[z, T_AT:ROWS, :] = rows
 
 
 def ladder_kernel(*refs):
-    out_ref, sa, sb, lhs, rhs, acc, wanted, names, lists_v, lists_s, sem = refs[10:]
+    out_ref, sa, sb, acc, wanted, plain, names, lists_v, lists_s, sem = refs[10:]
     my_x = lax.axis_index("x")
     blocks = [(ref, side, *(((0, 0, 8), (3, 0, 8), (1, 0, 8), (2, 0, 4), (2, 4, 4))[i])) for side in range(2) for i, ref in enumerate(refs[side * 5 : side * 5 + 5])]
     me = ((lax.axis_index("z") * 4) + lax.axis_index("x")) * 2 + lax.axis_index("core")
@@ -68,15 +79,13 @@
 
     at = 0
     for ref, _, _, _, size in blocks:
-        for z in range(0, size, 2):
-            for kind in range(3):
-                rows = [ref[z + i, T_AT + kind * MEMBERS : T_AT + (kind + 1) * MEMBERS, :] for i in range(2)]
-                rows = jnp.concatenate(rows, axis=0)
-                if kind == 2:
-                    wanted[at : at + 2 * MEMBERS, :] = rows
-                else:
-                    names[at : at + 2 * MEMBERS, kind * TB : (kind + 1) * TB] = rows.astype(jnp.bfloat16)
-            at += 2 * MEMBERS
+        for z in range(size):
+            for kind, table in enumerate((plain.at[0], plain.at[1], wanted)):
+                rows = ref[z, T_AT + kind * LIST_ROWS : T_AT + (kind + 1) * LIST_ROWS, :]
+                table[at : at + LIST_ROWS, :] = rows
+            at += LIST_ROWS
+    for kind in range(2):
+        names[:, kind * TB : (kind + 1) * TB] = plain[kind].astype(jnp.bfloat16)
 
     upto = lax.broadcasted_iota(jnp.int32, (TB, TB), 0) <= lax.broadcasted_iota(jnp.int32, (TB, TB), 1)
     upto = upto.astype(jnp.bfloat16)
@@ -95,11 +104,11 @@
         for t in range(TILES):
             carry = jnp.zeros((8, 1), jnp.float32)
             upper = []
-            pieces = [totals[t][:, i * TB : (i + 1) * TB] for i in range(LISTS // TB)]
-            within = [dot(piece.astype(jnp.bfloat16), upto) for piece in pieces]
-            for i in range(LISTS // TB):
-                upper.append(within[i] + carry)
-                carry = carry + within[i][:, TB - 1 : TB]
+            for i in range(0, LISTS, TB):
+                piece = totals[t][:, i : i + TB].astype(jnp.bfloat16)
+                within = dot(piece, upto[: piece.shape[1], : piece.shape[1]])
+                upper.append(within + carry)
+                carry = carry + within[:, -1:]
             uppers.append(jnp.concatenate(upper, axis=1))
             lowers.append(uppers[t] - totals[t])
             sums.append(carry)
@@ -115,8 +124,9 @@
             left = dot(ones, jnp.where(chosen, found[t][:, 0:TB], 0.0).astype(jnp.bfloat16), NT)
             right = dot(ones, jnp.where(chosen, found[t][:, TB : 2 * TB], 0.0).astype(jnp.bfloat16), NT)
             code = jnp.where(entry < sums[t], left * 256.0 + right, float(ALL_TILES * 256))
-            lists_v[t : t + 1, :] = code[0:1].astype(jnp.int32)
-            lists_v[TILES + t : TILES + t + 1, :] = jnp.broadcast_to(sums[t][0:1], (1, CHUNK)).astype(jnp.int32)
+            lists_v[t : t + 1, 0:CHUNK] = code[0:1].astype(jnp.int32)
+            lists_v[t : t + 1, CHUNK:] = jnp.full((1, WIDTH - CHUNK), ALL_TILES * 256, jnp.int32)
+            lists_v[TILES + t : TILES + t + 1, :] = jnp.broadcast_to(sums[t][0:1], (1, WIDTH)).astype(jnp.int32)
 
     def spread(index, _):
         for ref, side, step, first, size in blocks:
@@ -149,23 +159,33 @@
             acc[...] = jnp.zeros_like(acc)
 
         copy.wait()
-        most = lists_s[TILES, 0]
-        for t in range(1, TILES):
-            most = jnp.maximum(most, lists_s[TILES + t, 0])
+        most, starts = jnp.int32(0), [jnp.int32(0)]
+        for t in range(TILES):
+            total = lists_s[TILES + t, 0]
+            most = jnp.maximum(most, total)
+            starts.append(starts[t] + (jnp.clip(total - base, 0, CHUNK) + SUB - 1) // SUB)
 
         def block(index, _):
-            for t in range(TILES):
+            targets, sums = [], []
+            for u in range(WAYS):
+                at = index * WAYS + u
+                t = (at >= starts[1]).astype(jnp.int32) + (at >= starts[2]).astype(jnp.int32) + (at >= starts[3]).astype(jnp.int32)
+                first = jnp.where(t == 0, 0, jnp.where(t == 1, starts[1], jnp.where(t == 2, starts[2], starts[3])))
+                first = (at - first) * SUB
+                targets.append(t)
+                lefts, rights = [], []
                 for i in range(SUB):
-                    code = lists_s[t, index * SUB + i]
+                    code = lists_s[t, first + i]
                     a = pl.multiple_of((code >> 8) * KS, KS)
                     b = pl.multiple_of((code & 255) * KS, KS)
-                    lhs[t, i * KS : (i + 1) * KS, :] = sa[pl.ds(a, KS), :]
-                    rhs[t, i * KS : (i + 1) * KS, :] = sb[pl.ds(b, KS), :]
-            for t in range(TILES):
-                acc[t] += dot(lhs[t], rhs[t], TN)
+                    lefts.append(sa[pl.ds(a, KS), :])
+                    rights.append(sb[pl.ds(b, KS), :])
+                sums.append(dot(jnp.concatenate(lefts, axis=0), jnp.concatenate(rights, axis=0), TN))
+            for u in range(WAYS):
+                acc[targets[u]] += sums[u]
             return 0
 
-        lax.fori_loop(0, (jnp.clip(most - base, 0, CHUNK) + SUB - 1) // SUB, block, 0)
+        lax.fori_loop(0, (starts[TILES] + WAYS - 1) // WAYS, block, 0)
         return turn + 1, (most + CHUNK - 1) // CHUNK
 
     lax.while_loop(lambda s: s[0] < s[1], one_round, (jnp.int32(0), jnp.int32(1)))
@@ -192,24 +212,25 @@
     f32 = jnp.float32
     lists = pl.pallas_call(
         task_kernel,
-        out_shape=jax.ShapeDtypeStruct((MEMBERS, 3, TB), f32),
+        out_shape=pltpu.VMEM((MEMBERS, 3, TB), f32),
         in_specs=[VMEM, SMEM, VMEM, VMEM, VMEM],
         out_specs=VMEM,
     )(task_lists.transpose(0, 3, 1, 2), task_counts, amp_wanted, int_wanted, res_targets)
     lists = swap(lists, "grp")
     tiles = pl.pallas_call(
         turn_kernel,
-        out_shape=jax.ShapeDtypeStruct((T_AT, TB), f32),
+        out_shape=pltpu.VMEM((T_AT, TB), f32),
         in_specs=[VMEM] * 2,
         out_specs=VMEM,
         scratch_shapes=[pltpu.VMEM((TILES, TB, TB), f32)],
     )(amplitudes, integrals)
     payload = pl.pallas_call(
         payload_kernel,
-        out_shape=jax.ShapeDtypeStruct((8, ROWS, TB), f32),
-        in_specs=[VMEM] * 2,
-        out_specs=VMEM,
-    )(tiles, lists)
+        out_shape=pltpu.VMEM((8, ROWS, TB), f32),
+        in_specs=[SMEM, VMEM, VMEM],
+        out_specs=VMEM,
+        scratch_shapes=[pltpu.VMEM((MEMBERS, 3, TB), f32)],
+    )(task_counts, pltpu.with_memory_space_constraint(tiles, pltpu.VMEM), pltpu.with_memory_space_constraint(lists, pltpu.VMEM))
     here = swap(payload, "z")
     left, right = shift(here, 1), shift(here, -1)
     near = [here, left, right, shift(left[:4], 1), shift(right[4:], -1)]
@@ -217,19 +238,18 @@
     bf16 = jnp.bfloat16
     partial = pl.pallas_call(
         ladder_kernel,
-        out_shape=jax.ShapeDtypeStruct((MEMBERS, TILES, KS, TB), f32),
+        out_shape=pltpu.VMEM((MEMBERS, TILES, KS, TB), f32),
         in_specs=[VMEM] * 10,
         out_specs=VMEM,
         scratch_shapes=[
             pltpu.VMEM(((ALL_TILES + 1) * KS, 2 * TB), bf16),
             pltpu.VMEM((ALL_TILES * KS, 2 * TB), bf16),
-            pltpu.VMEM((TILES, SUB * KS, 2 * TB), bf16),
-            pltpu.VMEM((TILES, SUB * KS, 2 * TB), bf16),
             pltpu.VMEM((TILES, 2 * TB, 2 * TB), f32),
             pltpu.VMEM((LISTS, TB), f32),
+            pltpu.VMEM((2, LISTS, TB), f32),
             pltpu.VMEM((LISTS, (2 + TILES) * TB), bf16),
-            pltpu.VMEM((2 * TILES, CHUNK), jnp.int32),
-            pltpu.SMEM((2 * TILES, CHUNK), jnp.int32),
+            pltpu.VMEM((2 * TILES, WIDTH), jnp.int32),
+            pltpu.SMEM((2 * TILES, WIDTH), jnp.int32),
             pltpu.SemaphoreType.DMA,
         ],
         compiler_params=PARAMS,

time: 123 us -> 119 us (0.967)
  Pallas kernels: 14.4 us -> 12.2 us
    pallas_call x4, Pallas kernels: 14.4 us -> 12.2 us  [the longest x1 8.61 us: local(): pl.pallas_call(ladder_kernel, out_shape=pltpu.VMEM((MEMBERS, TILES, KS, T...]
  transfers between devices with their start and end apart: 11 -> 11, of which waited for: 4 -> 4; matrix products, arithmetic and copies ran while one was open for 0% -> 0% of each run, Pallas kernels for 2% -> 1%
where the time goes in v3:
time: 119 us; the launch traced here: 118 us
  starting transfers between devices  44.5 us (37%)
  blocking collectives  40.2 us (34%)
  waiting for transfers between devices  19.8 us (17%)
  Pallas kernels  12.2 us (10%)
    all_to_all x2, blocking collectives, swap(): return lax.all_to_all(block, axis, split_axis=0, concat_axis=0, tiled=True)  40.2 us
    ppermute x5, starting transfers between devices, local(): far = [lax.ppermute(block, 'core', [(0, 1), (1, 0)]) for block in near]  20.4 us
    all_to_all x2, waiting for transfers between devices, swap(): return lax.all_to_all(block, axis, split_axis=0, concat_axis=0, tiled=True)  17.7 us
    ppermute x4, starting transfers between devices, shift(): return lax.ppermute(block, 'x', [(i, (i + by) % 4) for i in range(4)])  13 us
    all_to_all x2, starting transfers between devices, swap(): return lax.all_to_all(block, axis, split_axis=0, concat_axis=0, tiled=True)  11.1 us
    pallas_call x1, Pallas kernels, local(): pl.pallas_call(ladder_kernel, out_shape=pltpu.VMEM((MEMBERS, TILES, KS, T...  8.61 us
  transfers between devices with their start and end apart: 11, of which 4 were waited for; matrix products, arithmetic and copies ran while one was open for 0% of the time, Pallas kernels for 1%

profile of v3, /device:TPU:1, one launch (start us, length us, event | category | flops | bytes accessed | tf_op | source)
XLA Modules:
  0.0 118.4 jit_solution(14273121715095229895)
XLA Ops:
  0.0 1.5 %shard_map.83 = f32[8,3,128]{2,1,0:T(4,128)} custom-call(s32[1,3,1,128]{3,2,1,0:T(1,128)} %bitcast.4, s32[1,8]{1,0:T(1,128)} %counts_ref.3, s32[1,64]{1,0:T(1,128)} %amp_ref.3, s32[1,64]{1,0:T(1,128)} %int_ref.3, s32[1,64]{1,0:T(1,128)} %res_ref.1), custom_call_target="tpu_custom_call" | custom-call | tf_op jit(solution)/shard_map/pallas_call | solution.py:213
  1.5 7.7 %all-to-all-start = ((f32[8,3,128]{2,1,0:T(4,128)}), f32[8,3,128]{2,1,0:T(4,128)S(1)}, u32[]{:S(2)}, u32[]{:S(2)}) async-start(f32[8,3,128]{2,1,0:T(4,128)} %shard_map.83), calls=%async_computation | async-start | bytes 32768 | tf_op jit(solution)/shard_map/all_to_all | solution.py:208
  9.2 1.2 %shard_map.82.tiles_ref = f32[128,128]{1,0:T(8,128)S(1)} custom-call(f32[4,128,128]{2,1,0:T(8,128)} %amp_ref.2, f32[4,128,128]{2,1,0:T(8,128)} %int_ref.2), custom_call_target="tpu_custom_call" | custom-call | tf_op jit(solution)/shard_map/pallas_call | solution.py:220
  10.4 5.4 %all-to-all-done.lists_ref = f32[8,3,128]{2,1,0:T(4,128)S(1)} async-done(((f32[8,3,128]{2,1,0:T(4,128)}), f32[8,3,128]{2,1,0:T(4,128)S(1)}, u32[]{:S(2)}, u32[]{:S(2)}) %all-to-all-start) | async-done | bytes 12320 | tf_op jit(solution)/shard_map/all_to_all | solution.py:208
  15.8 0.8 shard_map.84
  16.6 25.5 %all_to_all.20.refs_0_ = f32[8,144,128]{2,1,0:T(8,128)S(1)} all-to-all(f32[8,144,128]{2,1,0:T(8,128)S(1)} %shard_map.84), channel_id=1, replica_groups=mesh['z'=8,'x'=4,'core'=2,'grp'=8] {'z'}, dimensions={0} | all-to-all | bytes 1179648 | tf_op jit(solution)/shard_map/all_to_all | solution.py:208
  42.1 3.1 %collective-permute-start = (f32[8,144,128]{2,1,0:T(8,128)S(1)}, f32[8,144,128]{2,1,0:T(8,128)S(1)}, u32[]{:S(2)}, u32[]{:S(2)}) collective-permute-start(f32[8,144,128]{2,1,0:T(8,128)S(1)} %all_to_all.20.refs_0_), channel_id=1, source_target_pairs={{0,16},{16,32},{32,48},{48,0},{1,17},{17,33},{33,49},{49,1},{2,18}... | collective-permute-start | bytes 1769480 | tf_op jit(solution)/shard_map/ppermute | solution.py:204
  45.3 3.4 %collective-permute-start.1 = (f32[8,144,128]{2,1,0:T(8,128)S(1)}, f32[8,144,128]{2,1,0:T(8,128)S(1)}, u32[]{:S(2)}, u32[]{:S(2)}) collective-permute-start(f32[8,144,128]{2,1,0:T(8,128)S(1)} %all_to_all.20.refs_0_), channel_id=1, source_target_pairs={{0,48},{16,0},{32,16},{48,32},{1,49},{17,1},{33,17},{49,33},{2,50}... | collective-permute-start | bytes 1769480 | tf_op jit(solution)/shard_map/ppermute | solution.py:204
  48.6 6.6 %collective-permute-start.4 = (f32[8,144,128]{2,1,0:T(8,128)S(1)}, f32[8,144,128]{2,1,0:T(8,128)S(1)}, u32[]{:S(2)}, u32[]{:S(2)}) collective-permute-start(f32[8,144,128]{2,1,0:T(8,128)S(1)} %all_to_all.20.refs_0_), channel_id=1, source_target_pairs={{0,8},{8,0},{1,9},{9,1},{2,10},{10,2},{3,11},{11,3},{4,12},{12,4},... | collective-permute-start | bytes 1769480 | tf_op jit(solution)/shard_map/ppermute | solution.py:237
  55.3 0.6 collective-permute-done.refs_1_
  55.9 1.9 %collective-permute-start.2 = (f32[4,144,128]{2,1,0:T(8,128)S(1)}, f32[4,144,128]{2,1,0:T(8,128)S(1)}, u32[]{:S(2)}, u32[]{:S(2)}) collective-permute-start(f32[4,144,128]{2,1,0:T(8,128)S(1)} %slice.8), channel_id=1, source_target_pairs={{0,16},{16,32},{32,48},{48,0},{1,17},{17,33},{33,49},{49,1},{2,18}... | collective-permute-start | bytes 884744 | tf_op jit(solution)/shard_map/ppermute | solution.py:204
  57.9 0.0 collective-permute-done.1.refs_2_
  57.9 4.6 %collective-permute-start.3 = (f32[4,144,128]{2,1,0:T(8,128)S(1)}, f32[4,144,128]{2,1,0:T(8,128)S(1)}, u32[]{:S(2)}, u32[]{:S(2)}) collective-permute-start(f32[4,144,128]{2,1,0:T(8,128)S(1)} %slice.9), channel_id=1, source_target_pairs={{0,48},{16,0},{32,16},{48,32},{1,49},{17,1},{33,17},{49,33},{2,50}... | collective-permute-start | bytes 884744 | tf_op jit(solution)/shard_map/ppermute | solution.py:204
  62.5 7.5 %collective-permute-start.5 = (f32[8,144,128]{2,1,0:T(8,128)S(1)}, f32[8,144,128]{2,1,0:T(8,128)S(1)}, u32[]{:S(2)}, u32[]{:S(2)}) collective-permute-start(f32[8,144,128]{2,1,0:T(8,128)S(1)} %collective-permute-done.refs_1_), channel_id=1, source_target_pairs={{0,8},{8,0},{1,9},{9,1},{2,10},{10,2},{3,11},{11,3},{4,12},{12,4},... | collective-permute-start | bytes 1769480 | tf_op jit(solution)/shard_map/ppermute | solution.py:237
  70.0 1.9 %collective-permute-start.6 = (f32[8,144,128]{2,1,0:T(8,128)S(1)}, f32[8,144,128]{2,1,0:T(8,128)S(1)}, u32[]{:S(2)}, u32[]{:S(2)}) collective-permute-start(f32[8,144,128]{2,1,0:T(8,128)S(1)} %collective-permute-done.1.refs_2_), channel_id=1, source_target_pairs={{0,8},{8,0},{1,9},{9,1},{2,10},{10,2},{3,11},{11,3},{4,12},{12,4},... | collective-permute-start | bytes 1769480 | tf_op jit(solution)/shard_map/ppermute | solution.py:237
  72.0 0.0 collective-permute-done.2.refs_3_
  72.0 2.4 %collective-permute-start.7 = (f32[4,144,128]{2,1,0:T(8,128)S(1)}, f32[4,144,128]{2,1,0:T(8,128)S(1)}, u32[]{:S(2)}, u32[]{:S(2)}) collective-permute-start(f32[4,144,128]{2,1,0:T(8,128)S(1)} %collective-permute-done.2.refs_3_), channel_id=1, source_target_pairs={{0,8},{8,0},{1,9},{9,1},{2,10},{10,2},{3,11},{11,3},{4,12},{12,4},... | collective-permute-start | bytes 884744 | tf_op jit(solution)/shard_map/ppermute | solution.py:237
  74.4 0.0 collective-permute-done.3.refs_4_
  74.4 1.9 %collective-permute-start.8 = (f32[4,144,128]{2,1,0:T(8,128)S(1)}, f32[4,144,128]{2,1,0:T(8,128)S(1)}, u32[]{:S(2)}, u32[]{:S(2)}) collective-permute-start(f32[4,144,128]{2,1,0:T(8,128)S(1)} %collective-permute-done.3.refs_4_), channel_id=1, source_target_pairs={{0,8},{8,0},{1,9},{9,1},{2,10},{10,2},{3,11},{11,3},{4,12},{12,4},... | collective-permute-start | bytes 884744 | tf_op jit(solution)/shard_map/ppermute | solution.py:237
  76.3 0.0 collective-permute-done.4.refs_5_
  76.3 0.0 collective-permute-done.7.refs_8_
  76.3 1.5 %collective-permute-done.8.refs_9_ = f32[4,144,128]{2,1,0:T(8,128)S(1)} collective-permute-done((f32[4,144,128]{2,1,0:T(8,128)S(1)}, f32[4,144,128]{2,1,0:T(8,128)S(1)}, u32[]{:S(2)}, u32[]{:S(2)}) %collective-permute-start.8) | collective-permute-done | bytes 294944 | tf_op jit(solution)/shard_map/ppermute | solution.py:237
  77.9 0.0 collective-permute-done.5.refs_6_
  77.9 0.0 collective-permute-done.6.refs_7_
  77.9 8.6 %shard_map.85 = f32[8,4,16,128]{3,2,1,0:T(8,128)} custom-call(f32[8,144,128]{2,1,0:T(8,128)S(1)} %all_to_all.20.refs_0_, f32[8,144,128]{2,1,0:T(8,128)S(1)} %collective-permute-done.refs_1_, f32[8,144,128]{2,1,0:T(8,128)S(1)} %collective-permute-done.1.refs_2_, f32[4,144,128]{2,1,0:T(8,128)S(1)} %collective-permute-done.2.refs_3_, ...), custom_call_target="tpu_custom_call" | custom-call | tf_op jit(solution)/shard_map/pallas_call | solution.py:239
  86.5 3.4 %all-to-all-start.2 = ((f32[8,4,16,128]{3,2,1,0:T(8,128)}), f32[8,4,16,128]{3,2,1,0:T(8,128)S(1)}, u32[]{:S(2)}, u32[]{:S(2)}) async-start(f32[8,4,16,128]{3,2,1,0:T(8,128)} %shard_map.85), calls=%async_computation.2 | async-start | bytes 524288 | tf_op jit(solution)/shard_map/all_to_all | solution.py:208
  89.9 12.3 %all-to-all-done.2 = f32[8,4,16,128]{3,2,1,0:T(8,128)S(1)} async-done(((f32[8,4,16,128]{3,2,1,0:T(8,128)}), f32[8,4,16,128]{3,2,1,0:T(8,128)S(1)}, u32[]{:S(2)}, u32[]{:S(2)}) %all-to-all-start.2) | async-done | bytes 262176 | tf_op jit(solution)/shard_map/all_to_all | solution.py:208
  102.2 0.8 dynamic-slice_add_fusion
  103.0 14.7 %all_to_all.21 = f32[8,4,16,128]{3,2,1,0:T(8,128)S(1)} all-to-all(f32[8,4,16,128]{3,2,1,0:T(8,128)S(1)} %broadcast_in_dim.2), channel_id=1, replica_groups=mesh['z'=8,'x'=4,'core'=2,'grp'=8] {'grp'}, dimensions={0} | all-to-all | bytes 524288 | tf_op jit(solution)/shard_map/all_to_all | solution.py:208
  117.7 0.7 copy.9
  (4 shorter events, 0.1 us)
Async XLA Ops:
  1.5 14.3 %all-to-all-start = ((f32[8,3,128]{2,1,0:T(4,128)}), f32[8,3,128]{2,1,0:T(4,128)S(1)}, u32[]{:S(2)}, u32[]{:S(2)}) async-start(f32[8,3,128]{2,1,0:T(4,128)} %shard_map.83), calls=%async_computation | async-start | bytes 32768 | tf_op jit(solution)/shard_map/all_to_all | solution.py:208
  42.1 13.8 %collective-permute-start = (f32[8,144,128]{2,1,0:T(8,128)S(1)}, f32[8,144,128]{2,1,0:T(8,128)S(1)}, u32[]{:S(2)}, u32[]{:S(2)}) collective-permute-start(f32[8,144,128]{2,1,0:T(8,128)S(1)} %all_to_all.20.refs_0_), channel_id=1, source_target_pairs={{0,16},{16,32},{32,48},{48,0},{1,17},{17,33},{33,49},{49,1},{2,18}... | collective-permute-start | bytes 1769480 | tf_op jit(solution)/shard_map/ppermute | solution.py:204
  45.3 12.6 %collective-permute-start.1 = (f32[8,144,128]{2,1,0:T(8,128)S(1)}, f32[8,144,128]{2,1,0:T(8,128)S(1)}, u32[]{:S(2)}, u32[]{:S(2)}) collective-permute-start(f32[8,144,128]{2,1,0:T(8,128)S(1)} %all_to_all.20.refs_0_), channel_id=1, source_target_pairs={{0,48},{16,0},{32,16},{48,32},{1,49},{17,1},{33,17},{49,33},{2,50}... | collective-permute-start | bytes 1769480 | tf_op jit(solution)/shard_map/ppermute | solution.py:204
  48.6 27.7 %collective-permute-start.4 = (f32[8,144,128]{2,1,0:T(8,128)S(1)}, f32[8,144,128]{2,1,0:T(8,128)S(1)}, u32[]{:S(2)}, u32[]{:S(2)}) collective-permute-start(f32[8,144,128]{2,1,0:T(8,128)S(1)} %all_to_all.20.refs_0_), channel_id=1, source_target_pairs={{0,8},{8,0},{1,9},{9,1},{2,10},{10,2},{3,11},{11,3},{4,12},{12,4},... | collective-permute-start | bytes 1769480 | tf_op jit(solution)/shard_map/ppermute | solution.py:237
  55.9 16.0 %collective-permute-start.2 = (f32[4,144,128]{2,1,0:T(8,128)S(1)}, f32[4,144,128]{2,1,0:T(8,128)S(1)}, u32[]{:S(2)}, u32[]{:S(2)}) collective-permute-start(f32[4,144,128]{2,1,0:T(8,128)S(1)} %slice.8), channel_id=1, source_target_pairs={{0,16},{16,32},{32,48},{48,0},{1,17},{17,33},{33,49},{49,1},{2,18}... | collective-permute-start | bytes 884744 | tf_op jit(solution)/shard_map/ppermute | solution.py:204
  57.9 16.5 %collective-permute-start.3 = (f32[4,144,128]{2,1,0:T(8,128)S(1)}, f32[4,144,128]{2,1,0:T(8,128)S(1)}, u32[]{:S(2)}, u32[]{:S(2)}) collective-permute-start(f32[4,144,128]{2,1,0:T(8,128)S(1)} %slice.9), channel_id=1, source_target_pairs={{0,48},{16,0},{32,16},{48,32},{1,49},{17,1},{33,17},{49,33},{2,50}... | collective-permute-start | bytes 884744 | tf_op jit(solution)/shard_map/ppermute | solution.py:204
  62.5 15.4 %collective-permute-start.5 = (f32[8,144,128]{2,1,0:T(8,128)S(1)}, f32[8,144,128]{2,1,0:T(8,128)S(1)}, u32[]{:S(2)}, u32[]{:S(2)}) collective-permute-start(f32[8,144,128]{2,1,0:T(8,128)S(1)} %collective-permute-done.refs_1_), channel_id=1, source_target_pairs={{0,8},{8,0},{1,9},{9,1},{2,10},{10,2},{3,11},{11,3},{4,12},{12,4},... | collective-permute-start | bytes 1769480 | tf_op jit(solution)/shard_map/ppermute | solution.py:237
  70.0 7.8 %collective-permute-start.6 = (f32[8,144,128]{2,1,0:T(8,128)S(1)}, f32[8,144,128]{2,1,0:T(8,128)S(1)}, u32[]{:S(2)}, u32[]{:S(2)}) collective-permute-start(f32[8,144,128]{2,1,0:T(8,128)S(1)} %collective-permute-done.1.refs_2_), channel_id=1, source_target_pairs={{0,8},{8,0},{1,9},{9,1},{2,10},{10,2},{3,11},{11,3},{4,12},{12,4},... | collective-permute-start | bytes 1769480 | tf_op jit(solution)/shard_map/ppermute | solution.py:237
  72.0 4.4 %collective-permute-start.7 = (f32[4,144,128]{2,1,0:T(8,128)S(1)}, f32[4,144,128]{2,1,0:T(8,128)S(1)}, u32[]{:S(2)}, u32[]{:S(2)}) collective-permute-start(f32[4,144,128]{2,1,0:T(8,128)S(1)} %collective-permute-done.2.refs_3_), channel_id=1, source_target_pairs={{0,8},{8,0},{1,9},{9,1},{2,10},{10,2},{3,11},{11,3},{4,12},{12,4},... | collective-permute-start | bytes 884744 | tf_op jit(solution)/shard_map/ppermute | solution.py:237
  74.4 3.5 %collective-permute-start.8 = (f32[4,144,128]{2,1,0:T(8,128)S(1)}, f32[4,144,128]{2,1,0:T(8,128)S(1)}, u32[]{:S(2)}, u32[]{:S(2)}) collective-permute-start(f32[4,144,128]{2,1,0:T(8,128)S(1)} %collective-permute-done.3.refs_4_), channel_id=1, source_target_pairs={{0,8},{8,0},{1,9},{9,1},{2,10},{10,2},{3,11},{11,3},{4,12},{12,4},... | collective-permute-start | bytes 884744 | tf_op jit(solution)/shard_map/ppermute | solution.py:237
  86.5 15.7 %all-to-all-start.2 = ((f32[8,4,16,128]{3,2,1,0:T(8,128)}), f32[8,4,16,128]{3,2,1,0:T(8,128)S(1)}, u32[]{:S(2)}, u32[]{:S(2)}) async-start(f32[8,4,16,128]{3,2,1,0:T(8,128)} %shard_map.85), calls=%async_computation.2 | async-start | bytes 524288 | tf_op jit(solution)/shard_map/all_to_all | solution.py:208

commit v4 on v3

--- a/solution.py
+++ b/solution.py
@@ -15,10 +15,10 @@
 LIST_ROWS = 5
 A_AT, B_AT, T_AT = 0, TILES * KS, 2 * TILES * KS
 LISTS = OWNERS * LIST_ROWS
-CHUNK = 256
+CHUNK = 288
 SUB = 32
 WAYS = 3
-WIDTH = CHUNK + 128
+WIDTH = CHUNK + 96
 
 NT = (((1,), (1,)), ((), ()))
 TN = (((0,), (0,)), ((), ()))
@@ -71,15 +71,14 @@
 
 
 def ladder_kernel(*refs):
-    out_ref, sa, sb, acc, wanted, plain, names, lists_v, lists_s, sem = refs[10:]
-    my_x = lax.axis_index("x")
-    blocks = [(ref, side, *(((0, 0, 8), (3, 0, 8), (1, 0, 8), (2, 0, 4), (2, 4, 4))[i])) for side in range(2) for i, ref in enumerate(refs[side * 5 : side * 5 + 5])]
+    blocks, (out_ref, sa, sb, acc, wanted, plain, names, lists_v, lists_s, sem) = refs[:8], refs[8:]
     me = ((lax.axis_index("z") * 4) + lax.axis_index("x")) * 2 + lax.axis_index("core")
     core = lax.axis_index("core")
+    my_x = lax.axis_index("x")
 
     at = 0
-    for ref, _, _, _, size in blocks:
-        for z in range(size):
+    for ref in blocks:
+        for z in range(8):
             for kind, table in enumerate((plain.at[0], plain.at[1], wanted)):
                 rows = ref[z, T_AT + kind * LIST_ROWS : T_AT + (kind + 1) * LIST_ROWS, :]
                 table[at : at + LIST_ROWS, :] = rows
@@ -128,22 +127,19 @@
             lists_v[t : t + 1, CHUNK:] = jnp.full((1, WIDTH - CHUNK), ALL_TILES * 256, jnp.int32)
             lists_v[TILES + t : TILES + t + 1, :] = jnp.broadcast_to(sums[t][0:1], (1, WIDTH)).astype(jnp.int32)
 
-    def spread(index, _):
-        for ref, side, step, first, size in blocks:
-            if size == 4:
-                ref = ref.at[pl.ds(index // 2, 1)]
-            else:
-                ref = ref.at[pl.ds(index, 1)]
-            z = index // 2 + first if size == 4 else index
-            c = core if side == 0 else 1 - core
-            owner = (z * 4 + (my_x + step) % 4) * 2 + c
+    def spread(z):
+        for i, ref in enumerate(blocks):
+            c = core if i < 4 else 1 - core
+            owner = (z * 4 + (my_x + (0, 3, 1, 2)[i % 4]) % 4) * 2 + c
             to = pl.ds(pl.multiple_of(owner * TILES * KS, TILES * KS), TILES * KS)
             for at, store in ((A_AT, sa), (B_AT, sb)):
-                value = ref[0, at : at + TILES * KS, :]
+                value = ref[z, at : at + TILES * KS, :]
+                if store is sa:
+                    store[to, :] = value
+                    continue
                 high = value.astype(jnp.bfloat16)
                 store[to, 0:TB] = high
                 store[to, TB : 2 * TB] = (value - high.astype(jnp.float32)).astype(jnp.bfloat16)
-        return 0
 
     def one_round(state):
         turn, _ = state
@@ -154,8 +150,9 @@
 
         @pl.when(turn == 0)
         def _():
-            lax.fori_loop(0, 8, spread, 0)
-            sa[ALL_TILES * KS :, :] = jnp.zeros((KS, 2 * TB), jnp.bfloat16)
+            for z in range(8):
+                spread(z)
+            sa[ALL_TILES * KS :, :] = jnp.zeros((KS, TB), jnp.float32)
             acc[...] = jnp.zeros_like(acc)
 
         copy.wait()
@@ -180,7 +177,10 @@
                     b = pl.multiple_of((code & 255) * KS, KS)
                     lefts.append(sa[pl.ds(a, KS), :])
                     rights.append(sb[pl.ds(b, KS), :])
-                sums.append(dot(jnp.concatenate(lefts, axis=0), jnp.concatenate(rights, axis=0), TN))
+                turned = jnp.concatenate(lefts, axis=0).T
+                high = turned.astype(jnp.bfloat16)
+                turned = jnp.concatenate([high, (turned - high.astype(jnp.float32)).astype(jnp.bfloat16)], axis=0)
+                sums.append(dot(turned, jnp.concatenate(rights, axis=0)))
             for u in range(WAYS):
                 acc[targets[u]] += sums[u]
             return 0
@@ -191,8 +191,8 @@
     lax.while_loop(lambda s: s[0] < s[1], one_round, (jnp.int32(0), jnp.int32(1)))
     for t in range(TILES):
         total = (acc[t, 0:TB, 0:TB] + acc[t, 0:TB, TB:]) + (acc[t, TB:, 0:TB] + acc[t, TB:, TB:])
-        for m in range(MEMBERS):
-            out_ref[m, t] = total[m * KS : (m + 1) * KS, :]
+        for half in range(2):
+            out_ref[2 * t + half] = total[half * TB // 2 : (half + 1) * TB // 2, :]
 
 
 VMEM = pl.BlockSpec(memory_space=pltpu.VMEM)
@@ -202,6 +202,10 @@
 
 def shift(block, by):
     return lax.ppermute(block, "x", [(i, (i + by) % 4) for i in range(4)])
+
+
+def across(block):
+    return lax.ppermute(block, "core", [(0, 1), (1, 0)])
 
 
 def swap(block, axis):
@@ -232,17 +236,19 @@
         scratch_shapes=[pltpu.VMEM((MEMBERS, 3, TB), f32)],
     )(task_counts, pltpu.with_memory_space_constraint(tiles, pltpu.VMEM), pltpu.with_memory_space_constraint(lists, pltpu.VMEM))
     here = swap(payload, "z")
-    left, right = shift(here, 1), shift(here, -1)
-    near = [here, left, right, shift(left[:4], 1), shift(right[4:], -1)]
-    far = [lax.ppermute(block, "core", [(0, 1), (1, 0)]) for block in near]
+    left, right, here_far = shift(here, 1), shift(here, -1), across(here)
+    ahead, behind, here_far = lax.optimization_barrier((shift(left[:4], 1), shift(right[4:], -1), here_far))
+    opposite = jnp.concatenate([ahead, behind])
+    near = [here, left, right, opposite]
+    far = [here_far, across(left), across(right), across(opposite)]
     bf16 = jnp.bfloat16
     partial = pl.pallas_call(
         ladder_kernel,
-        out_shape=pltpu.VMEM((MEMBERS, TILES, KS, TB), f32),
-        in_specs=[VMEM] * 10,
+        out_shape=pltpu.VMEM((MEMBERS, TB // 2, TB), f32),
+        in_specs=[VMEM] * 8,
         out_specs=VMEM,
         scratch_shapes=[
-            pltpu.VMEM(((ALL_TILES + 1) * KS, 2 * TB), bf16),
+            pltpu.VMEM(((ALL_TILES + 1) * KS, TB), f32),
             pltpu.VMEM((ALL_TILES * KS, 2 * TB), bf16),
             pltpu.VMEM((TILES, 2 * TB, 2 * TB), f32),
             pltpu.VMEM((LISTS, TB), f32),
@@ -254,11 +260,11 @@
         ],
         compiler_params=PARAMS,
     )(*near, *far)
-    member = lax.axis_index("grp")
-    rows = lax.dynamic_slice_in_dim(residual_in, member * KS, KS, 1)
-    rows = rows + jnp.sum(swap(partial, "grp"), axis=0)
-    whole = swap(jnp.broadcast_to(rows[None], (MEMBERS, TILES, KS, TB)), "grp")
-    return whole.transpose(1, 0, 2, 3).reshape(TILES, TB, TB)
+    halves = residual_in.reshape(MEMBERS, TB // 2, TB)
+    half = lax.dynamic_index_in_dim(halves, lax.axis_index("grp"), 0, keepdims=False)
+    half = half + jnp.sum(swap(partial, "grp"), axis=0)
+    whole = swap(jnp.broadcast_to(half[None], halves.shape), "grp")
+    return whole.reshape(TILES, TB, TB)
 
 
 def solution(mesh):

time: 119 us -> 116 us (0.975)
  starting transfers between devices: 44.5 us -> 42.6 us
    ppermute x5 -> x4, starting transfers between devices: 20.4 us -> 18.5 us  [across(): return lax.ppermute(block, 'core', [(0, 1), (1, 0)])]
  transfers between devices with their start and end apart: 11 -> 10, of which waited for: 4 -> 4; matrix products, arithmetic and copies ran while one was open for 0% -> 0% of each run, Pallas kernels for 1% -> 1%
where the time goes in v4:
time: 116 us
  starting transfers between devices  42.6 us (37%)
  blocking collectives  40.2 us (35%)
  waiting for transfers between devices  19.9 us (17%)
  Pallas kernels  11.4 us (10%)
    all_to_all x2, blocking collectives, swap(): return lax.all_to_all(block, axis, split_axis=0, concat_axis=0, tiled=True)  40.2 us
    ppermute x4, starting transfers between devices, across(): return lax.ppermute(block, 'core', [(0, 1), (1, 0)])  18.5 us
    all_to_all x2, waiting for transfers between devices, swap(): return lax.all_to_all(block, axis, split_axis=0, concat_axis=0, tiled=True)  17.7 us
    ppermute x4, starting transfers between devices, shift(): return lax.ppermute(block, 'x', [(i, (i + by) % 4) for i in range(4)])  13 us
    all_to_all x2, starting transfers between devices, swap(): return lax.all_to_all(block, axis, split_axis=0, concat_axis=0, tiled=True)  11.1 us
    pallas_call x1, Pallas kernels, local(): pl.pallas_call(ladder_kernel, out_shape=pltpu.VMEM((MEMBERS, TB // 2, TB)...  7.82 us
  transfers between devices with their start and end apart: 10, of which 4 were waited for; matrix products, arithmetic and copies ran while one was open for 0% of the time, Pallas kernels for 1%

profile of v4, /device:TPU:1, one launch (start us, length us, event | category | flops | bytes accessed | tf_op | source)
XLA Modules:
  0.0 115.8 jit_solution(9381303928654396584)
XLA Ops:
  0.0 1.5 %shard_map.83 = f32[8,3,128]{2,1,0:T(4,128)} custom-call(s32[1,3,1,128]{3,2,1,0:T(1,128)} %bitcast.11, s32[1,8]{1,0:T(1,128)} %counts_ref.3, s32[1,64]{1,0:T(1,128)} %amp_ref.3, s32[1,64]{1,0:T(1,128)} %int_ref.3, s32[1,64]{1,0:T(1,128)} %res_ref.1), custom_call_target="tpu_custom_call" | custom-call | tf_op jit(solution)/shard_map/pallas_call | solution.py:217
  1.5 7.7 %all-to-all-start = ((f32[8,3,128]{2,1,0:T(4,128)}), f32[8,3,128]{2,1,0:T(4,128)S(1)}, u32[]{:S(2)}, u32[]{:S(2)}) async-start(f32[8,3,128]{2,1,0:T(4,128)} %shard_map.83), calls=%async_computation | async-start | bytes 32768 | tf_op jit(solution)/shard_map/all_to_all | solution.py:212
  9.2 1.2 %shard_map.82.tiles_ref = f32[128,128]{1,0:T(8,128)S(1)} custom-call(f32[4,128,128]{2,1,0:T(8,128)} %amp_ref.2, f32[4,128,128]{2,1,0:T(8,128)} %int_ref.2), custom_call_target="tpu_custom_call" | custom-call | tf_op jit(solution)/shard_map/pallas_call | solution.py:224
  10.4 5.4 %all-to-all-done.lists_ref = f32[8,3,128]{2,1,0:T(4,128)S(1)} async-done(((f32[8,3,128]{2,1,0:T(4,128)}), f32[8,3,128]{2,1,0:T(4,128)S(1)}, u32[]{:S(2)}, u32[]{:S(2)}) %all-to-all-start) | async-done | bytes 12320 | tf_op jit(solution)/shard_map/all_to_all | solution.py:212
  15.8 0.8 shard_map.84
  16.6 25.5 %all_to_all.20.refs_0_ = f32[8,144,128]{2,1,0:T(8,128)S(1)} all-to-all(f32[8,144,128]{2,1,0:T(8,128)S(1)} %shard_map.84), channel_id=1, replica_groups=mesh['z'=8,'x'=4,'core'=2,'grp'=8] {'z'}, dimensions={0} | all-to-all | bytes 1179648 | tf_op jit(solution)/shard_map/all_to_all | solution.py:212
  42.1 3.1 %collective-permute-start = (f32[8,144,128]{2,1,0:T(8,128)S(1)}, f32[8,144,128]{2,1,0:T(8,128)S(1)}, u32[]{:S(2)}, u32[]{:S(2)}) collective-permute-start(f32[8,144,128]{2,1,0:T(8,128)S(1)} %all_to_all.20.refs_0_), channel_id=1, source_target_pairs={{0,16},{16,32},{32,48},{48,0},{1,17},{17,33},{33,49},{49,1},{2,18}... | collective-permute-start | bytes 1769480 | tf_op jit(solution)/shard_map/ppermute | solution.py:204
  45.3 3.4 %collective-permute-start.1 = (f32[8,144,128]{2,1,0:T(8,128)S(1)}, f32[8,144,128]{2,1,0:T(8,128)S(1)}, u32[]{:S(2)}, u32[]{:S(2)}) collective-permute-start(f32[8,144,128]{2,1,0:T(8,128)S(1)} %all_to_all.20.refs_0_), channel_id=1, source_target_pairs={{0,48},{16,0},{32,16},{48,32},{1,49},{17,1},{33,17},{49,33},{2,50}... | collective-permute-start | bytes 1769480 | tf_op jit(solution)/shard_map/ppermute | solution.py:204
  48.6 6.6 %collective-permute-start.4 = (f32[8,144,128]{2,1,0:T(8,128)S(1)}, f32[8,144,128]{2,1,0:T(8,128)S(1)}, u32[]{:S(2)}, u32[]{:S(2)}) collective-permute-start(f32[8,144,128]{2,1,0:T(8,128)S(1)} %all_to_all.20.refs_0_), channel_id=1, source_target_pairs={{0,8},{8,0},{1,9},{9,1},{2,10},{10,2},{3,11},{11,3},{4,12},{12,4},... | collective-permute-start | bytes 1769480 | tf_op jit(solution)/shard_map/ppermute | solution.py:208
  55.3 0.6 collective-permute-done.refs_1_
  55.9 1.9 %collective-permute-start.2 = (f32[4,144,128]{2,1,0:T(8,128)S(1)}, f32[4,144,128]{2,1,0:T(8,128)S(1)}, u32[]{:S(2)}, u32[]{:S(2)}) collective-permute-start(f32[4,144,128]{2,1,0:T(8,128)S(1)} %slice.8), channel_id=1, source_target_pairs={{0,16},{16,32},{32,48},{48,0},{1,17},{17,33},{33,49},{49,1},{2,18}... | collective-permute-start | bytes 884744 | tf_op jit(solution)/shard_map/ppermute | solution.py:204
  57.9 0.0 collective-permute-done.1.refs_2_
  57.9 4.6 %collective-permute-start.3 = (f32[4,144,128]{2,1,0:T(8,128)S(1)}, f32[4,144,128]{2,1,0:T(8,128)S(1)}, u32[]{:S(2)}, u32[]{:S(2)}) collective-permute-start(f32[4,144,128]{2,1,0:T(8,128)S(1)} %slice.9), channel_id=1, source_target_pairs={{0,48},{16,0},{32,16},{48,32},{1,49},{17,1},{33,17},{49,33},{2,50}... | collective-permute-start | bytes 884744 | tf_op jit(solution)/shard_map/ppermute | solution.py:204
  62.5 7.5 %collective-permute-start.5 = (f32[8,144,128]{2,1,0:T(8,128)S(1)}, f32[8,144,128]{2,1,0:T(8,128)S(1)}, u32[]{:S(2)}, u32[]{:S(2)}) collective-permute-start(f32[8,144,128]{2,1,0:T(8,128)S(1)} %collective-permute-done.refs_1_), channel_id=1, source_target_pairs={{0,8},{8,0},{1,9},{9,1},{2,10},{10,2},{3,11},{11,3},{4,12},{12,4},... | collective-permute-start | bytes 1769480 | tf_op jit(solution)/shard_map/ppermute | solution.py:208
  70.0 1.9 %collective-permute-start.6 = (f32[8,144,128]{2,1,0:T(8,128)S(1)}, f32[8,144,128]{2,1,0:T(8,128)S(1)}, u32[]{:S(2)}, u32[]{:S(2)}) collective-permute-start(f32[8,144,128]{2,1,0:T(8,128)S(1)} %collective-permute-done.1.refs_2_), channel_id=1, source_target_pairs={{0,8},{8,0},{1,9},{9,1},{2,10},{10,2},{3,11},{11,3},{4,12},{12,4},... | collective-permute-start | bytes 1769480 | tf_op jit(solution)/shard_map/ppermute | solution.py:208
  72.0 0.0 collective-permute-done.4.refs_4_
  72.0 0.0 collective-permute-done.2
  72.0 0.0 collective-permute-done.3
  72.1 2.4 %collective-permute-start.7 = (f32[8,144,128]{2,1,0:T(8,128)S(1)}, f32[8,144,128]{2,1,0:T(8,128)S(1)}, u32[]{:S(2)}, u32[]{:S(2)}) collective-permute-start(f32[8,144,128]{2,1,0:T(8,128)S(1)} %constant_dynamic-update-slice_fusion.refs_3_), channel_id=1, source_target_pairs={{0,8},{8,0},{1,9},{9,1},{2,10},{10,2},{3,11},{11,3},{4,12},{12,4},... | collective-permute-start | bytes 1769480 | tf_op jit(solution)/shard_map/ppermute | solution.py:208
  74.5 0.0 collective-permute-done.5.refs_5_
  74.5 0.0 collective-permute-done.6.refs_6_
  74.5 1.6 %collective-permute-done.7.refs_7_ = f32[8,144,128]{2,1,0:T(8,128)S(1)} collective-permute-done((f32[8,144,128]{2,1,0:T(8,128)S(1)}, f32[8,144,128]{2,1,0:T(8,128)S(1)}, u32[]{:S(2)}, u32[]{:S(2)}) %collective-permute-start.7) | collective-permute-done | bytes 589856 | tf_op jit(solution)/shard_map/ppermute | solution.py:208
  76.1 7.8 %shard_map.85 = f32[8,64,128]{2,1,0:T(8,128)} custom-call(f32[8,144,128]{2,1,0:T(8,128)S(1)} %all_to_all.20.refs_0_, f32[8,144,128]{2,1,0:T(8,128)S(1)} %collective-permute-done.refs_1_, f32[8,144,128]{2,1,0:T(8,128)S(1)} %collective-permute-done.1.refs_2_, f32[8,144,128]{2,1,0:T(8,128)S(1)} %constant_dynamic-update-slice_fusion.refs_3_, ...), custom_call_target="tpu_custom_call" | custom-call | tf_op jit(solution)/shard_map/pallas_call | solution.py:245
  83.9 3.4 %all-to-all-start.2 = ((f32[8,64,128]{2,1,0:T(8,128)}), f32[8,64,128]{2,1,0:T(8,128)S(1)}, u32[]{:S(2)}, u32[]{:S(2)}) async-start(f32[8,64,128]{2,1,0:T(8,128)} %shard_map.85), calls=%async_computation.2 | async-start | bytes 524288 | tf_op jit(solution)/shard_map/all_to_all | solution.py:212
  87.3 12.3 %all-to-all-done.2 = f32[8,64,128]{2,1,0:T(8,128)S(1)} async-done(((f32[8,64,128]{2,1,0:T(8,128)}), f32[8,64,128]{2,1,0:T(8,128)S(1)}, u32[]{:S(2)}, u32[]{:S(2)}) %all-to-all-start.2) | async-done | bytes 262176 | tf_op jit(solution)/shard_map/all_to_all | solution.py:212
  99.6 0.8 fusion
  100.4 14.6 %all_to_all.21 = f32[8,64,128]{2,1,0:T(8,128)S(1)} all-to-all(f32[8,64,128]{2,1,0:T(8,128)S(1)} %broadcast_in_dim.9), channel_id=1, replica_groups=mesh['z'=8,'x'=4,'core'=2,'grp'=8] {'grp'}, dimensions={0} | all-to-all | bytes 524288 | tf_op jit(solution)/shard_map/all_to_all | solution.py:212
  115.1 0.7 copy.11
  (6 shorter events, 0.1 us)
Async XLA Ops:
  1.5 14.3 %all-to-all-start = ((f32[8,3,128]{2,1,0:T(4,128)}), f32[8,3,128]{2,1,0:T(4,128)S(1)}, u32[]{:S(2)}, u32[]{:S(2)}) async-start(f32[8,3,128]{2,1,0:T(4,128)} %shard_map.83), calls=%async_computation | async-start | bytes 32768 | tf_op jit(solution)/shard_map/all_to_all | solution.py:212
  42.1 13.8 %collective-permute-start = (f32[8,144,128]{2,1,0:T(8,128)S(1)}, f32[8,144,128]{2,1,0:T(8,128)S(1)}, u32[]{:S(2)}, u32[]{:S(2)}) collective-permute-start(f32[8,144,128]{2,1,0:T(8,128)S(1)} %all_to_all.20.refs_0_), channel_id=1, source_target_pairs={{0,16},{16,32},{32,48},{48,0},{1,17},{17,33},{33,49},{49,1},{2,18}... | collective-permute-start | bytes 1769480 | tf_op jit(solution)/shard_map/ppermute | solution.py:204
  45.3 12.6 %collective-permute-start.1 = (f32[8,144,128]{2,1,0:T(8,128)S(1)}, f32[8,144,128]{2,1,0:T(8,128)S(1)}, u32[]{:S(2)}, u32[]{:S(2)}) collective-permute-start(f32[8,144,128]{2,1,0:T(8,128)S(1)} %all_to_all.20.refs_0_), channel_id=1, source_target_pairs={{0,48},{16,0},{32,16},{48,32},{1,49},{17,1},{33,17},{49,33},{2,50}... | collective-permute-start | bytes 1769480 | tf_op jit(solution)/shard_map/ppermute | solution.py:204
  48.6 23.3 %collective-permute-start.4 = (f32[8,144,128]{2,1,0:T(8,128)S(1)}, f32[8,144,128]{2,1,0:T(8,128)S(1)}, u32[]{:S(2)}, u32[]{:S(2)}) collective-permute-start(f32[8,144,128]{2,1,0:T(8,128)S(1)} %all_to_all.20.refs_0_), channel_id=1, source_target_pairs={{0,8},{8,0},{1,9},{9,1},{2,10},{10,2},{3,11},{11,3},{4,12},{12,4},... | collective-permute-start | bytes 1769480 | tf_op jit(solution)/shard_map/ppermute | solution.py:208
  55.9 16.0 %collective-permute-start.2 = (f32[4,144,128]{2,1,0:T(8,128)S(1)}, f32[4,144,128]{2,1,0:T(8,128)S(1)}, u32[]{:S(2)}, u32[]{:S(2)}) collective-permute-start(f32[4,144,128]{2,1,0:T(8,128)S(1)} %slice.8), channel_id=1, source_target_pairs={{0,16},{16,32},{32,48},{48,0},{1,17},{17,33},{33,49},{49,1},{2,18}... | collective-permute-start | bytes 884744 | tf_op jit(solution)/shard_map/ppermute | solution.py:204
  57.9 14.1 %collective-permute-start.3 = (f32[4,144,128]{2,1,0:T(8,128)S(1)}, f32[4,144,128]{2,1,0:T(8,128)S(1)}, u32[]{:S(2)}, u32[]{:S(2)}) collective-permute-start(f32[4,144,128]{2,1,0:T(8,128)S(1)} %slice.9), channel_id=1, source_target_pairs={{0,48},{16,0},{32,16},{48,32},{1,49},{17,1},{33,17},{49,33},{2,50}... | collective-permute-start | bytes 884744 | tf_op jit(solution)/shard_map/ppermute | solution.py:204
  62.5 12.0 %collective-permute-start.5 = (f32[8,144,128]{2,1,0:T(8,128)S(1)}, f32[8,144,128]{2,1,0:T(8,128)S(1)}, u32[]{:S(2)}, u32[]{:S(2)}) collective-permute-start(f32[8,144,128]{2,1,0:T(8,128)S(1)} %collective-permute-done.refs_1_), channel_id=1, source_target_pairs={{0,8},{8,0},{1,9},{9,1},{2,10},{10,2},{3,11},{11,3},{4,12},{12,4},... | collective-permute-start | bytes 1769480 | tf_op jit(solution)/shard_map/ppermute | solution.py:208
  70.0 4.4 %collective-permute-start.6 = (f32[8,144,128]{2,1,0:T(8,128)S(1)}, f32[8,144,128]{2,1,0:T(8,128)S(1)}, u32[]{:S(2)}, u32[]{:S(2)}) collective-permute-start(f32[8,144,128]{2,1,0:T(8,128)S(1)} %collective-permute-done.1.refs_2_), channel_id=1, source_target_pairs={{0,8},{8,0},{1,9},{9,1},{2,10},{10,2},{3,11},{11,3},{4,12},{12,4},... | collective-permute-start | bytes 1769480 | tf_op jit(solution)/shard_map/ppermute | solution.py:208
  72.1 4.0 %collective-permute-start.7 = (f32[8,144,128]{2,1,0:T(8,128)S(1)}, f32[8,144,128]{2,1,0:T(8,128)S(1)}, u32[]{:S(2)}, u32[]{:S(2)}) collective-permute-start(f32[8,144,128]{2,1,0:T(8,128)S(1)} %constant_dynamic-update-slice_fusion.refs_3_), channel_id=1, source_target_pairs={{0,8},{8,0},{1,9},{9,1},{2,10},{10,2},{3,11},{11,3},{4,12},{12,4},... | collective-permute-start | bytes 1769480 | tf_op jit(solution)/shard_map/ppermute | solution.py:208
  83.9 15.7 %all-to-all-start.2 = ((f32[8,64,128]{2,1,0:T(8,128)}), f32[8,64,128]{2,1,0:T(8,128)S(1)}, u32[]{:S(2)}, u32[]{:S(2)}) async-start(f32[8,64,128]{2,1,0:T(8,128)} %shard_map.85), calls=%async_computation.2 | async-start | bytes 524288 | tf_op jit(solution)/shard_map/all_to_all | solution.py:212

commit v5 on v4

--- a/solution.py
+++ b/solution.py
@@ -71,7 +71,9 @@
 
 
 def ladder_kernel(*refs):
-    blocks, (out_ref, sa, sb, acc, wanted, plain, names, lists_v, lists_s, sem) = refs[:8], refs[8:]
+    parts, (out_ref, sa, sb, acc, wanted, plain, names, lists_v, lists_s, sem) = refs[:10], refs[10:]
+    blocks = [[[ref.at[z] for z in range(8)] for ref in parts[i : i + 3]] + [[parts[i + 3 + z // 4].at[z % 4] for z in range(8)]] for i in (0, 5)]
+    blocks = blocks[0] + blocks[1]
     me = ((lax.axis_index("z") * 4) + lax.axis_index("x")) * 2 + lax.axis_index("core")
     core = lax.axis_index("core")
     my_x = lax.axis_index("x")
@@ -80,7 +82,7 @@
     for ref in blocks:
         for z in range(8):
             for kind, table in enumerate((plain.at[0], plain.at[1], wanted)):
-                rows = ref[z, T_AT + kind * LIST_ROWS : T_AT + (kind + 1) * LIST_ROWS, :]
+                rows = ref[z][T_AT + kind * LIST_ROWS : T_AT + (kind + 1) * LIST_ROWS, :]
                 table[at : at + LIST_ROWS, :] = rows
             at += LIST_ROWS
     for kind in range(2):
@@ -133,7 +135,7 @@
             owner = (z * 4 + (my_x + (0, 3, 1, 2)[i % 4]) % 4) * 2 + c
             to = pl.ds(pl.multiple_of(owner * TILES * KS, TILES * KS), TILES * KS)
             for at, store in ((A_AT, sa), (B_AT, sb)):
-                value = ref[z, at : at + TILES * KS, :]
+                value = ref[z][at : at + TILES * KS, :]
                 if store is sa:
                     store[to, :] = value
                     continue
@@ -236,16 +238,14 @@
         scratch_shapes=[pltpu.VMEM((MEMBERS, 3, TB), f32)],
     )(task_counts, pltpu.with_memory_space_constraint(tiles, pltpu.VMEM), pltpu.with_memory_space_constraint(lists, pltpu.VMEM))
     here = swap(payload, "z")
-    left, right, here_far = shift(here, 1), shift(here, -1), across(here)
-    ahead, behind, here_far = lax.optimization_barrier((shift(left[:4], 1), shift(right[4:], -1), here_far))
-    opposite = jnp.concatenate([ahead, behind])
-    near = [here, left, right, opposite]
-    far = [here_far, across(left), across(right), across(opposite)]
+    left, right = shift(here, 1), shift(here, -1)
+    near = [here, left, right, shift(left[:4], 1), shift(right[4:], -1)]
+    far = [across(block) for block in near]
     bf16 = jnp.bfloat16
     partial = pl.pallas_call(
         ladder_kernel,
         out_shape=pltpu.VMEM((MEMBERS, TB // 2, TB), f32),
-        in_specs=[VMEM] * 8,
+        in_specs=[VMEM] * 10,
         out_specs=VMEM,
         scratch_shapes=[
             pltpu.VMEM(((ALL_TILES + 1) * KS, TB), f32),

time: 116 us -> 118 us (1.017)
  starting transfers between devices: 42.6 us -> 44.5 us
    ppermute x4 -> x5, starting transfers between devices: 18.5 us -> 20.4 us  [across(): return lax.ppermute(block, 'core', [(0, 1), (1, 0)])]
  transfers between devices with their start and end apart: 10 -> 11, of which waited for: 4 -> 4; matrix products, arithmetic and copies ran while one was open for 0% -> 0% of each run, Pallas kernels for 1% -> 1%
where the time goes in v5:
time: 118 us
  starting transfers between devices  44.5 us (38%)
  blocking collectives  40.2 us (34%)
  waiting for transfers between devices  19.8 us (17%)
  Pallas kernels  11.4 us (10%)
    all_to_all x2, blocking collectives, swap(): return lax.all_to_all(block, axis, split_axis=0, concat_axis=0, tiled=True)  40.2 us
    ppermute x5, starting transfers between devices, across(): return lax.ppermute(block, 'core', [(0, 1), (1, 0)])  20.4 us
    all_to_all x2, waiting for transfers between devices, swap(): return lax.all_to_all(block, axis, split_axis=0, concat_axis=0, tiled=True)  17.7 us
    ppermute x4, starting transfers between devices, shift(): return lax.ppermute(block, 'x', [(i, (i + by) % 4) for i in range(4)])  13 us
    all_to_all x2, starting transfers between devices, swap(): return lax.all_to_all(block, axis, split_axis=0, concat_axis=0, tiled=True)  11.1 us
    pallas_call x1, Pallas kernels, local(): pl.pallas_call(ladder_kernel, out_shape=pltpu.VMEM((MEMBERS, TB // 2, TB)...  7.83 us
  transfers between devices with their start and end apart: 11, of which 4 were waited for; matrix products, arithmetic and copies ran while one was open for 0% of the time, Pallas kernels for 1%

profile of v5, /device:TPU:1, one launch (start us, length us, event | category | flops | bytes accessed | tf_op | source)
XLA Modules:
  0.0 117.6 jit_solution(3378562655217724509)
XLA Ops:
  0.0 1.5 %shard_map.83 = f32[8,3,128]{2,1,0:T(4,128)} custom-call(s32[1,3,1,128]{3,2,1,0:T(1,128)} %bitcast.11, s32[1,8]{1,0:T(1,128)} %counts_ref.3, s32[1,64]{1,0:T(1,128)} %amp_ref.3, s32[1,64]{1,0:T(1,128)} %int_ref.3, s32[1,64]{1,0:T(1,128)} %res_ref.1), custom_call_target="tpu_custom_call" | custom-call | tf_op jit(solution)/shard_map/pallas_call | solution.py:219
  1.5 7.7 %all-to-all-start = ((f32[8,3,128]{2,1,0:T(4,128)}), f32[8,3,128]{2,1,0:T(4,128)S(1)}, u32[]{:S(2)}, u32[]{:S(2)}) async-start(f32[8,3,128]{2,1,0:T(4,128)} %shard_map.83), calls=%async_computation | async-start | bytes 32768 | tf_op jit(solution)/shard_map/all_to_all | solution.py:214
  9.2 1.2 %shard_map.82.tiles_ref = f32[128,128]{1,0:T(8,128)S(1)} custom-call(f32[4,128,128]{2,1,0:T(8,128)} %amp_ref.2, f32[4,128,128]{2,1,0:T(8,128)} %int_ref.2), custom_call_target="tpu_custom_call" | custom-call | tf_op jit(solution)/shard_map/pallas_call | solution.py:226
  10.4 5.4 %all-to-all-done.lists_ref = f32[8,3,128]{2,1,0:T(4,128)S(1)} async-done(((f32[8,3,128]{2,1,0:T(4,128)}), f32[8,3,128]{2,1,0:T(4,128)S(1)}, u32[]{:S(2)}, u32[]{:S(2)}) %all-to-all-start) | async-done | bytes 12320 | tf_op jit(solution)/shard_map/all_to_all | solution.py:214
  15.8 0.8 shard_map.84
  16.6 25.5 %all_to_all.20.refs_0_ = f32[8,144,128]{2,1,0:T(8,128)S(1)} all-to-all(f32[8,144,128]{2,1,0:T(8,128)S(1)} %shard_map.84), channel_id=1, replica_groups=mesh['z'=8,'x'=4,'core'=2,'grp'=8] {'z'}, dimensions={0} | all-to-all | bytes 1179648 | tf_op jit(solution)/shard_map/all_to_all | solution.py:214
  42.1 3.1 %collective-permute-start = (f32[8,144,128]{2,1,0:T(8,128)S(1)}, f32[8,144,128]{2,1,0:T(8,128)S(1)}, u32[]{:S(2)}, u32[]{:S(2)}) collective-permute-start(f32[8,144,128]{2,1,0:T(8,128)S(1)} %all_to_all.20.refs_0_), channel_id=1, source_target_pairs={{0,16},{16,32},{32,48},{48,0},{1,17},{17,33},{33,49},{49,1},{2,18}... | collective-permute-start | bytes 1769480 | tf_op jit(solution)/shard_map/ppermute | solution.py:206
  45.3 3.4 %collective-permute-start.1 = (f32[8,144,128]{2,1,0:T(8,128)S(1)}, f32[8,144,128]{2,1,0:T(8,128)S(1)}, u32[]{:S(2)}, u32[]{:S(2)}) collective-permute-start(f32[8,144,128]{2,1,0:T(8,128)S(1)} %all_to_all.20.refs_0_), channel_id=1, source_target_pairs={{0,48},{16,0},{32,16},{48,32},{1,49},{17,1},{33,17},{49,33},{2,50}... | collective-permute-start | bytes 1769480 | tf_op jit(solution)/shard_map/ppermute | solution.py:206
  48.6 6.6 %collective-permute-start.4 = (f32[8,144,128]{2,1,0:T(8,128)S(1)}, f32[8,144,128]{2,1,0:T(8,128)S(1)}, u32[]{:S(2)}, u32[]{:S(2)}) collective-permute-start(f32[8,144,128]{2,1,0:T(8,128)S(1)} %all_to_all.20.refs_0_), channel_id=1, source_target_pairs={{0,8},{8,0},{1,9},{9,1},{2,10},{10,2},{3,11},{11,3},{4,12},{12,4},... | collective-permute-start | bytes 1769480 | tf_op jit(solution)/shard_map/ppermute | solution.py:210
  55.3 0.6 collective-permute-done.refs_1_
  55.9 1.9 %collective-permute-start.2 = (f32[4,144,128]{2,1,0:T(8,128)S(1)}, f32[4,144,128]{2,1,0:T(8,128)S(1)}, u32[]{:S(2)}, u32[]{:S(2)}) collective-permute-start(f32[4,144,128]{2,1,0:T(8,128)S(1)} %slice.8), channel_id=1, source_target_pairs={{0,16},{16,32},{32,48},{48,0},{1,17},{17,33},{33,49},{49,1},{2,18}... | collective-permute-start | bytes 884744 | tf_op jit(solution)/shard_map/ppermute | solution.py:206
  57.9 0.0 collective-permute-done.1.refs_2_
  57.9 4.6 %collective-permute-start.3 = (f32[4,144,128]{2,1,0:T(8,128)S(1)}, f32[4,144,128]{2,1,0:T(8,128)S(1)}, u32[]{:S(2)}, u32[]{:S(2)}) collective-permute-start(f32[4,144,128]{2,1,0:T(8,128)S(1)} %slice.9), channel_id=1, source_target_pairs={{0,48},{16,0},{32,16},{48,32},{1,49},{17,1},{33,17},{49,33},{2,50}... | collective-permute-start | bytes 884744 | tf_op jit(solution)/shard_map/ppermute | solution.py:206
  62.5 7.5 %collective-permute-start.5 = (f32[8,144,128]{2,1,0:T(8,128)S(1)}, f32[8,144,128]{2,1,0:T(8,128)S(1)}, u32[]{:S(2)}, u32[]{:S(2)}) collective-permute-start(f32[8,144,128]{2,1,0:T(8,128)S(1)} %collective-permute-done.refs_1_), channel_id=1, source_target_pairs={{0,8},{8,0},{1,9},{9,1},{2,10},{10,2},{3,11},{11,3},{4,12},{12,4},... | collective-permute-start | bytes 1769480 | tf_op jit(solution)/shard_map/ppermute | solution.py:210
  70.0 1.9 %collective-permute-start.6 = (f32[8,144,128]{2,1,0:T(8,128)S(1)}, f32[8,144,128]{2,1,0:T(8,128)S(1)}, u32[]{:S(2)}, u32[]{:S(2)}) collective-permute-start(f32[8,144,128]{2,1,0:T(8,128)S(1)} %collective-permute-done.1.refs_2_), channel_id=1, source_target_pairs={{0,8},{8,0},{1,9},{9,1},{2,10},{10,2},{3,11},{11,3},{4,12},{12,4},... | collective-permute-start | bytes 1769480 | tf_op jit(solution)/shard_map/ppermute | solution.py:210
  72.0 0.0 collective-permute-done.2.refs_3_
  72.0 2.4 %collective-permute-start.7 = (f32[4,144,128]{2,1,0:T(8,128)S(1)}, f32[4,144,128]{2,1,0:T(8,128)S(1)}, u32[]{:S(2)}, u32[]{:S(2)}) collective-permute-start(f32[4,144,128]{2,1,0:T(8,128)S(1)} %collective-permute-done.2.refs_3_), channel_id=1, source_target_pairs={{0,8},{8,0},{1,9},{9,1},{2,10},{10,2},{3,11},{11,3},{4,12},{12,4},... | collective-permute-start | bytes 884744 | tf_op jit(solution)/shard_map/ppermute | solution.py:210
  74.4 0.0 collective-permute-done.3.refs_4_
  74.4 1.9 %collective-permute-start.8 = (f32[4,144,128]{2,1,0:T(8,128)S(1)}, f32[4,144,128]{2,1,0:T(8,128)S(1)}, u32[]{:S(2)}, u32[]{:S(2)}) collective-permute-start(f32[4,144,128]{2,1,0:T(8,128)S(1)} %collective-permute-done.3.refs_4_), channel_id=1, source_target_pairs={{0,8},{8,0},{1,9},{9,1},{2,10},{10,2},{3,11},{11,3},{4,12},{12,4},... | collective-permute-start | bytes 884744 | tf_op jit(solution)/shard_map/ppermute | solution.py:210
  76.3 0.0 collective-permute-done.4.refs_5_
  76.3 0.0 collective-permute-done.7.refs_8_
  76.3 1.5 %collective-permute-done.8.refs_9_ = f32[4,144,128]{2,1,0:T(8,128)S(1)} collective-permute-done((f32[4,144,128]{2,1,0:T(8,128)S(1)}, f32[4,144,128]{2,1,0:T(8,128)S(1)}, u32[]{:S(2)}, u32[]{:S(2)}) %collective-permute-start.8) | collective-permute-done | bytes 294944 | tf_op jit(solution)/shard_map/ppermute | solution.py:210
  77.9 0.0 collective-permute-done.5.refs_6_
  77.9 0.0 collective-permute-done.6.refs_7_
  77.9 7.8 %shard_map.85 = f32[8,64,128]{2,1,0:T(8,128)} custom-call(f32[8,144,128]{2,1,0:T(8,128)S(1)} %all_to_all.20.refs_0_, f32[8,144,128]{2,1,0:T(8,128)S(1)} %collective-permute-done.refs_1_, f32[8,144,128]{2,1,0:T(8,128)S(1)} %collective-permute-done.1.refs_2_, f32[4,144,128]{2,1,0:T(8,128)S(1)} %collective-permute-done.2.refs_3_, ...), custom_call_target="tpu_custom_call" | custom-call | tf_op jit(solution)/shard_map/pallas_call | solution.py:245
  85.7 3.4 %all-to-all-start.2 = ((f32[8,64,128]{2,1,0:T(8,128)}), f32[8,64,128]{2,1,0:T(8,128)S(1)}, u32[]{:S(2)}, u32[]{:S(2)}) async-start(f32[8,64,128]{2,1,0:T(8,128)} %shard_map.85), calls=%async_computation.2 | async-start | bytes 524288 | tf_op jit(solution)/shard_map/all_to_all | solution.py:214
  89.2 12.3 %all-to-all-done.2 = f32[8,64,128]{2,1,0:T(8,128)S(1)} async-done(((f32[8,64,128]{2,1,0:T(8,128)}), f32[8,64,128]{2,1,0:T(8,128)S(1)}, u32[]{:S(2)}, u32[]{:S(2)}) %all-to-all-start.2) | async-done | bytes 262176 | tf_op jit(solution)/shard_map/all_to_all | solution.py:214
  101.5 0.8 fusion
  102.3 14.7 %all_to_all.21 = f32[8,64,128]{2,1,0:T(8,128)S(1)} all-to-all(f32[8,64,128]{2,1,0:T(8,128)S(1)} %broadcast_in_dim.9), channel_id=1, replica_groups=mesh['z'=8,'x'=4,'core'=2,'grp'=8] {'grp'}, dimensions={0} | all-to-all | bytes 524288 | tf_op jit(solution)/shard_map/all_to_all | solution.py:214
  116.9 0.7 copy.10
  (4 shorter events, 0.1 us)
Async XLA Ops:
  1.5 14.3 %all-to-all-start = ((f32[8,3,128]{2,1,0:T(4,128)}), f32[8,3,128]{2,1,0:T(4,128)S(1)}, u32[]{:S(2)}, u32[]{:S(2)}) async-start(f32[8,3,128]{2,1,0:T(4,128)} %shard_map.83), calls=%async_computation | async-start | bytes 32768 | tf_op jit(solution)/shard_map/all_to_all | solution.py:214
  42.1 13.8 %collective-permute-start = (f32[8,144,128]{2,1,0:T(8,128)S(1)}, f32[8,144,128]{2,1,0:T(8,128)S(1)}, u32[]{:S(2)}, u32[]{:S(2)}) collective-permute-start(f32[8,144,128]{2,1,0:T(8,128)S(1)} %all_to_all.20.refs_0_), channel_id=1, source_target_pairs={{0,16},{16,32},{32,48},{48,0},{1,17},{17,33},{33,49},{49,1},{2,18}... | collective-permute-start | bytes 1769480 | tf_op jit(solution)/shard_map/ppermute | solution.py:206
  45.3 12.6 %collective-permute-start.1 = (f32[8,144,128]{2,1,0:T(8,128)S(1)}, f32[8,144,128]{2,1,0:T(8,128)S(1)}, u32[]{:S(2)}, u32[]{:S(2)}) collective-permute-start(f32[8,144,128]{2,1,0:T(8,128)S(1)} %all_to_all.20.refs_0_), channel_id=1, source_target_pairs={{0,48},{16,0},{32,16},{48,32},{1,49},{17,1},{33,17},{49,33},{2,50}... | collective-permute-start | bytes 1769480 | tf_op jit(solution)/shard_map/ppermute | solution.py:206
  48.6 27.7 %collective-permute-start.4 = (f32[8,144,128]{2,1,0:T(8,128)S(1)}, f32[8,144,128]{2,1,0:T(8,128)S(1)}, u32[]{:S(2)}, u32[]{:S(2)}) collective-permute-start(f32[8,144,128]{2,1,0:T(8,128)S(1)} %all_to_all.20.refs_0_), channel_id=1, source_target_pairs={{0,8},{8,0},{1,9},{9,1},{2,10},{10,2},{3,11},{11,3},{4,12},{12,4},... | collective-permute-start | bytes 1769480 | tf_op jit(solution)/shard_map/ppermute | solution.py:210
  55.9 16.0 %collective-permute-start.2 = (f32[4,144,128]{2,1,0:T(8,128)S(1)}, f32[4,144,128]{2,1,0:T(8,128)S(1)}, u32[]{:S(2)}, u32[]{:S(2)}) collective-permute-start(f32[4,144,128]{2,1,0:T(8,128)S(1)} %slice.8), channel_id=1, source_target_pairs={{0,16},{16,32},{32,48},{48,0},{1,17},{17,33},{33,49},{49,1},{2,18}... | collective-permute-start | bytes 884744 | tf_op jit(solution)/shard_map/ppermute | solution.py:206
  57.9 16.5 %collective-permute-start.3 = (f32[4,144,128]{2,1,0:T(8,128)S(1)}, f32[4,144,128]{2,1,0:T(8,128)S(1)}, u32[]{:S(2)}, u32[]{:S(2)}) collective-permute-start(f32[4,144,128]{2,1,0:T(8,128)S(1)} %slice.9), channel_id=1, source_target_pairs={{0,48},{16,0},{32,16},{48,32},{1,49},{17,1},{33,17},{49,33},{2,50}... | collective-permute-start | bytes 884744 | tf_op jit(solution)/shard_map/ppermute | solution.py:206
  62.5 15.4 %collective-permute-start.5 = (f32[8,144,128]{2,1,0:T(8,128)S(1)}, f32[8,144,128]{2,1,0:T(8,128)S(1)}, u32[]{:S(2)}, u32[]{:S(2)}) collective-permute-start(f32[8,144,128]{2,1,0:T(8,128)S(1)} %collective-permute-done.refs_1_), channel_id=1, source_target_pairs={{0,8},{8,0},{1,9},{9,1},{2,10},{10,2},{3,11},{11,3},{4,12},{12,4},... | collective-permute-start | bytes 1769480 | tf_op jit(solution)/shard_map/ppermute | solution.py:210
  70.0 7.8 %collective-permute-start.6 = (f32[8,144,128]{2,1,0:T(8,128)S(1)}, f32[8,144,128]{2,1,0:T(8,128)S(1)}, u32[]{:S(2)}, u32[]{:S(2)}) collective-permute-start(f32[8,144,128]{2,1,0:T(8,128)S(1)} %collective-permute-done.1.refs_2_), channel_id=1, source_target_pairs={{0,8},{8,0},{1,9},{9,1},{2,10},{10,2},{3,11},{11,3},{4,12},{12,4},... | collective-permute-start | bytes 1769480 | tf_op jit(solution)/shard_map/ppermute | solution.py:210
  72.0 4.4 %collective-permute-start.7 = (f32[4,144,128]{2,1,0:T(8,128)S(1)}, f32[4,144,128]{2,1,0:T(8,128)S(1)}, u32[]{:S(2)}, u32[]{:S(2)}) collective-permute-start(f32[4,144,128]{2,1,0:T(8,128)S(1)} %collective-permute-done.2.refs_3_), channel_id=1, source_target_pairs={{0,8},{8,0},{1,9},{9,1},{2,10},{10,2},{3,11},{11,3},{4,12},{12,4},... | collective-permute-start | bytes 884744 | tf_op jit(solution)/shard_map/ppermute | solution.py:210
  74.4 3.5 %collective-permute-start.8 = (f32[4,144,128]{2,1,0:T(8,128)S(1)}, f32[4,144,128]{2,1,0:T(8,128)S(1)}, u32[]{:S(2)}, u32[]{:S(2)}) collective-permute-start(f32[4,144,128]{2,1,0:T(8,128)S(1)} %collective-permute-done.3.refs_4_), channel_id=1, source_target_pairs={{0,8},{8,0},{1,9},{9,1},{2,10},{10,2},{3,11},{11,3},{4,12},{12,4},... | collective-permute-start | bytes 884744 | tf_op jit(solution)/shard_map/ppermute | solution.py:210
  85.7 15.7 %all-to-all-start.2 = ((f32[8,64,128]{2,1,0:T(8,128)}), f32[8,64,128]{2,1,0:T(8,128)S(1)}, u32[]{:S(2)}, u32[]{:S(2)}) async-start(f32[8,64,128]{2,1,0:T(8,128)} %shard_map.85), calls=%async_computation.2 | async-start | bytes 524288 | tf_op jit(solution)/shard_map/all_to_all | solution.py:214

commit v6 on v4

--- a/solution.py
+++ b/solution.py
@@ -28,38 +28,38 @@
     return lax.dot_general(a, b, dims, preferred_element_type=jnp.float32)
 
 
-def task_kernel(tasks_ref, counts_ref, amp_ref, int_ref, res_ref, out_ref):
-    live = counts_ref[0, lax.axis_index("grp")]
+def turn_kernel(amp_ref, int_ref, out_ref, turned):
+    first = pl.multiple_of(lax.axis_index("grp") * KS, KS)
+    for at, tiles in ((A_AT, amp_ref), (B_AT, int_ref)):
+        for t in range(TILES):
+            turned[t] = tiles[t].T
+        for t in range(TILES):
+            out_ref[at + t * KS : at + (t + 1) * KS, :] = turned[t, pl.ds(first, KS), :]
+
+
+def payload_kernel(counts_ref, tiles_ref, lists_ref, amp_ref, int_ref, res_ref, out_ref, joined):
     owner = lax.broadcasted_iota(jnp.int32, (OWNERS, TB), 0)
     slot = lax.broadcasted_iota(jnp.int32, (OWNERS, TB), 1)
     number = lax.broadcasted_iota(jnp.int32, (8, OWNERS), 1) * TILES
-    for kind, table in enumerate((amp_ref, int_ref, res_ref)):
-        hit = tasks_ref[0, kind] == owner
-        if kind == 2:
-            hit = hit & (slot < live)
-        names = number + table[0:1, :] + (1 if kind == 2 else 0)
-        row = dot(names.astype(jnp.bfloat16), hit.astype(jnp.bfloat16))[0:1]
-        row = row - 1.0 if kind == 2 else row
-        for m in range(MEMBERS):
-            out_ref[m, kind : kind + 1, :] = row
-
-
-def turn_kernel(amp_ref, int_ref, out_ref, turned):
-    first = pl.multiple_of(lax.axis_index("grp") * KS, KS)
-    for at, tiles in ((A_AT, amp_ref), (B_AT, int_ref)):
-        for t in range(TILES):
-            turned[t] = tiles[t].T
-        for t in range(TILES):
-            out_ref[at + t * KS : at + (t + 1) * KS, :] = turned[t, pl.ds(first, KS), :]
-
-
-def payload_kernel(counts_ref, tiles_ref, lists_ref, out_ref, joined):
+
+    def named(m):
+        rows = []
+        for kind, table in enumerate((amp_ref, int_ref, res_ref)):
+            hit = lists_ref[m, kind : kind + 1, :] == owner
+            if kind == 2:
+                hit = hit & (slot < counts_ref[0, m])
+            names = number + table[0:1, :] + (1 if kind == 2 else 0)
+            row = dot(names.astype(jnp.bfloat16), hit.astype(jnp.bfloat16))[0:1]
+            rows.append(row - 1.0 if kind == 2 else row)
+        return jnp.concatenate(rows, axis=0)
+
+    lists = [named(m) for m in range(MEMBERS)]
     joined[...] = jnp.full_like(joined, -1.0)
     lane = lax.broadcasted_iota(jnp.int32, (3, TB), 1)
     at = jnp.int32(0)
     for m in range(MEMBERS):
         row, by = at // TB, at % TB
-        turned = pltpu.roll(lists_ref[m], by, 1)
+        turned = pltpu.roll(lists[m], by, 1)
         joined[row] = jnp.where(lane >= by, turned, joined[row])
         joined[row + 1] = jnp.where(lane < by, turned, joined[row + 1])
         at = at + counts_ref[0, m]
@@ -214,12 +214,7 @@
 
 def local(amplitudes, integrals, residual_in, task_lists, task_counts, amp_wanted, int_wanted, res_targets):
     f32 = jnp.float32
-    lists = pl.pallas_call(
-        task_kernel,
-        out_shape=pltpu.VMEM((MEMBERS, 3, TB), f32),
-        in_specs=[VMEM, SMEM, VMEM, VMEM, VMEM],
-        out_specs=VMEM,
-    )(task_lists.transpose(0, 3, 1, 2), task_counts, amp_wanted, int_wanted, res_targets)
+    lists = jnp.broadcast_to(task_lists.transpose(0, 3, 1, 2).reshape(1, 3, TB), (MEMBERS, 3, TB))
     lists = swap(lists, "grp")
     tiles = pl.pallas_call(
         turn_kernel,
@@ -231,10 +226,10 @@
     payload = pl.pallas_call(
         payload_kernel,
         out_shape=pltpu.VMEM((8, ROWS, TB), f32),
-        in_specs=[SMEM, VMEM, VMEM],
+        in_specs=[SMEM] + [VMEM] * 5,
         out_specs=VMEM,
         scratch_shapes=[pltpu.VMEM((MEMBERS, 3, TB), f32)],
-    )(task_counts, pltpu.with_memory_space_constraint(tiles, pltpu.VMEM), pltpu.with_memory_space_constraint(lists, pltpu.VMEM))
+    )(task_counts, pltpu.with_memory_space_constraint(tiles, pltpu.VMEM), pltpu.with_memory_space_constraint(lists, pltpu.VMEM), amp_wanted, int_wanted, res_targets)
     here = swap(payload, "z")
     left, right, here_far = shift(here, 1), shift(here, -1), across(here)
     ahead, behind, here_far = lax.optimization_barrier((shift(left[:4], 1), shift(right[4:], -1), here_far))

time: 116 us -> 117 us (level)
  local copies, waits for them, and re-layouts: 0.81 us -> 2.1 us
  Pallas kernels: 11.4 us -> 10.2 us
    pallas_call x1 -> x0, Pallas kernels: 1.54 us -> none  [local(): pl.pallas_call(task_kernel, out_shape=pltpu.VMEM((MEMBERS, 3, TB), f32),...]
where the time goes in v6:
time: 117 us; the launch traced here: 116 us
  starting transfers between devices  42.6 us (36%)
  blocking collectives  40.2 us (34%)
  waiting for transfers between devices  19.9 us (17%)
  Pallas kernels  10.2 us (9%)
  local copies, waits for them, and re-layouts  2.1 us (2%)
    all_to_all x2, blocking collectives, swap(): return lax.all_to_all(block, axis, split_axis=0, concat_axis=0, tiled=True)  40.2 us
    ppermute x4, starting transfers between devices, across(): return lax.ppermute(block, 'core', [(0, 1), (1, 0)])  18.5 us
    all_to_all x2, waiting for transfers between devices, swap(): return lax.all_to_all(block, axis, split_axis=0, concat_axis=0, tiled=True)  17.7 us
    ppermute x4, starting transfers between devices, shift(): return lax.ppermute(block, 'x', [(i, (i + by) % 4) for i in range(4)])  13 us
    all_to_all x2, starting transfers between devices, swap(): return lax.all_to_all(block, axis, split_axis=0, concat_axis=0, tiled=True)  11.1 us
    pallas_call x1, Pallas kernels, local(): pl.pallas_call(ladder_kernel, out_shape=pltpu.VMEM((MEMBERS, TB // 2, TB)...  7.82 us
  transfers between devices with their start and end apart: 10, of which 4 were waited for; matrix products, arithmetic and copies ran while one was open for 0% of the time, Pallas kernels for 1%

profile of v6, /device:TPU:1, one launch (start us, length us, event | category | flops | bytes accessed | tf_op | source)
XLA Modules:
  0.0 115.9 jit_solution(12650581962843238018)
XLA Ops:
  0.0 0.0 copy-start
  0.0 0.7 copy-done
  0.7 0.6 broadcast_in_dim.16
  1.3 7.7 %all-to-all-start = ((s32[8,3,128]{2,1,0:T(4,128)}), s32[8,3,128]{2,1,0:T(4,128)S(1)}, u32[]{:S(2)}, u32[]{:S(2)}) async-start(s32[8,3,128]{2,1,0:T(4,128)} %broadcast_in_dim.16), calls=%async_computation | async-start | bytes 32768 | tf_op jit(solution)/shard_map/all_to_all | solution.py:212
  8.9 1.2 %shard_map.82.tiles_ref = f32[128,128]{1,0:T(8,128)S(1)} custom-call(f32[4,128,128]{2,1,0:T(8,128)} %amp_ref.2, f32[4,128,128]{2,1,0:T(8,128)} %int_ref.2), custom_call_target="tpu_custom_call" | custom-call | tf_op jit(solution)/shard_map/pallas_call | solution.py:219
  10.2 5.4 %all-to-all-done.lists_ref = s32[8,3,128]{2,1,0:T(4,128)S(1)} async-done(((s32[8,3,128]{2,1,0:T(4,128)}), s32[8,3,128]{2,1,0:T(4,128)S(1)}, u32[]{:S(2)}, u32[]{:S(2)}) %all-to-all-start) | async-done | bytes 12320 | tf_op jit(solution)/shard_map/all_to_all | solution.py:212
  15.6 1.1 shard_map.83
  16.7 25.5 %all_to_all.20.refs_0_ = f32[8,144,128]{2,1,0:T(8,128)S(1)} all-to-all(f32[8,144,128]{2,1,0:T(8,128)S(1)} %shard_map.83), channel_id=1, replica_groups=mesh['z'=8,'x'=4,'core'=2,'grp'=8] {'z'}, dimensions={0} | all-to-all | bytes 1179648 | tf_op jit(solution)/shard_map/all_to_all | solution.py:212
  42.2 3.1 %collective-permute-start = (f32[8,144,128]{2,1,0:T(8,128)S(1)}, f32[8,144,128]{2,1,0:T(8,128)S(1)}, u32[]{:S(2)}, u32[]{:S(2)}) collective-permute-start(f32[8,144,128]{2,1,0:T(8,128)S(1)} %all_to_all.20.refs_0_), channel_id=1, source_target_pairs={{0,16},{16,32},{32,48},{48,0},{1,17},{17,33},{33,49},{49,1},{2,18}... | collective-permute-start | bytes 1769480 | tf_op jit(solution)/shard_map/ppermute | solution.py:204
  45.4 3.4 %collective-permute-start.1 = (f32[8,144,128]{2,1,0:T(8,128)S(1)}, f32[8,144,128]{2,1,0:T(8,128)S(1)}, u32[]{:S(2)}, u32[]{:S(2)}) collective-permute-start(f32[8,144,128]{2,1,0:T(8,128)S(1)} %all_to_all.20.refs_0_), channel_id=1, source_target_pairs={{0,48},{16,0},{32,16},{48,32},{1,49},{17,1},{33,17},{49,33},{2,50}... | collective-permute-start | bytes 1769480 | tf_op jit(solution)/shard_map/ppermute | solution.py:204
  48.7 6.6 %collective-permute-start.4 = (f32[8,144,128]{2,1,0:T(8,128)S(1)}, f32[8,144,128]{2,1,0:T(8,128)S(1)}, u32[]{:S(2)}, u32[]{:S(2)}) collective-permute-start(f32[8,144,128]{2,1,0:T(8,128)S(1)} %all_to_all.20.refs_0_), channel_id=1, source_target_pairs={{0,8},{8,0},{1,9},{9,1},{2,10},{10,2},{3,11},{11,3},{4,12},{12,4},... | collective-permute-start | bytes 1769480 | tf_op jit(solution)/shard_map/ppermute | solution.py:208
  55.4 0.6 collective-permute-done.refs_1_
  56.0 1.9 %collective-permute-start.2 = (f32[4,144,128]{2,1,0:T(8,128)S(1)}, f32[4,144,128]{2,1,0:T(8,128)S(1)}, u32[]{:S(2)}, u32[]{:S(2)}) collective-permute-start(f32[4,144,128]{2,1,0:T(8,128)S(1)} %slice.8), channel_id=1, source_target_pairs={{0,16},{16,32},{32,48},{48,0},{1,17},{17,33},{33,49},{49,1},{2,18}... | collective-permute-start | bytes 884744 | tf_op jit(solution)/shard_map/ppermute | solution.py:204
  58.0 0.0 collective-permute-done.1.refs_2_
  58.0 4.6 %collective-permute-start.3 = (f32[4,144,128]{2,1,0:T(8,128)S(1)}, f32[4,144,128]{2,1,0:T(8,128)S(1)}, u32[]{:S(2)}, u32[]{:S(2)}) collective-permute-start(f32[4,144,128]{2,1,0:T(8,128)S(1)} %slice.9), channel_id=1, source_target_pairs={{0,48},{16,0},{32,16},{48,32},{1,49},{17,1},{33,17},{49,33},{2,50}... | collective-permute-start | bytes 884744 | tf_op jit(solution)/shard_map/ppermute | solution.py:204
  62.6 7.5 %collective-permute-start.5 = (f32[8,144,128]{2,1,0:T(8,128)S(1)}, f32[8,144,128]{2,1,0:T(8,128)S(1)}, u32[]{:S(2)}, u32[]{:S(2)}) collective-permute-start(f32[8,144,128]{2,1,0:T(8,128)S(1)} %collective-permute-done.refs_1_), channel_id=1, source_target_pairs={{0,8},{8,0},{1,9},{9,1},{2,10},{10,2},{3,11},{11,3},{4,12},{12,4},... | collective-permute-start | bytes 1769480 | tf_op jit(solution)/shard_map/ppermute | solution.py:208
  70.1 1.9 %collective-permute-start.6 = (f32[8,144,128]{2,1,0:T(8,128)S(1)}, f32[8,144,128]{2,1,0:T(8,128)S(1)}, u32[]{:S(2)}, u32[]{:S(2)}) collective-permute-start(f32[8,144,128]{2,1,0:T(8,128)S(1)} %collective-permute-done.1.refs_2_), channel_id=1, source_target_pairs={{0,8},{8,0},{1,9},{9,1},{2,10},{10,2},{3,11},{11,3},{4,12},{12,4},... | collective-permute-start | bytes 1769480 | tf_op jit(solution)/shard_map/ppermute | solution.py:208
  72.1 0.0 collective-permute-done.4.refs_4_
  72.1 0.0 collective-permute-done.2
  72.1 0.0 collective-permute-done.3
  72.2 2.4 %collective-permute-start.7 = (f32[8,144,128]{2,1,0:T(8,128)S(1)}, f32[8,144,128]{2,1,0:T(8,128)S(1)}, u32[]{:S(2)}, u32[]{:S(2)}) collective-permute-start(f32[8,144,128]{2,1,0:T(8,128)S(1)} %constant_dynamic-update-slice_fusion.refs_3_), channel_id=1, source_target_pairs={{0,8},{8,0},{1,9},{9,1},{2,10},{10,2},{3,11},{11,3},{4,12},{12,4},... | collective-permute-start | bytes 1769480 | tf_op jit(solution)/shard_map/ppermute | solution.py:208
  74.6 0.0 collective-permute-done.5.refs_5_
  74.6 0.0 collective-permute-done.6.refs_6_
  74.6 1.6 %collective-permute-done.7.refs_7_ = f32[8,144,128]{2,1,0:T(8,128)S(1)} collective-permute-done((f32[8,144,128]{2,1,0:T(8,128)S(1)}, f32[8,144,128]{2,1,0:T(8,128)S(1)}, u32[]{:S(2)}, u32[]{:S(2)}) %collective-permute-start.7) | collective-permute-done | bytes 589856 | tf_op jit(solution)/shard_map/ppermute | solution.py:208
  76.2 7.8 %shard_map.84 = f32[8,64,128]{2,1,0:T(8,128)} custom-call(f32[8,144,128]{2,1,0:T(8,128)S(1)} %all_to_all.20.refs_0_, f32[8,144,128]{2,1,0:T(8,128)S(1)} %collective-permute-done.refs_1_, f32[8,144,128]{2,1,0:T(8,128)S(1)} %collective-permute-done.1.refs_2_, f32[8,144,128]{2,1,0:T(8,128)S(1)} %constant_dynamic-update-slice_fusion.refs_3_, ...), custom_call_target="tpu_custom_call" | custom-call | tf_op jit(solution)/shard_map/pallas_call | solution.py:240
  84.0 3.4 %all-to-all-start.2 = ((f32[8,64,128]{2,1,0:T(8,128)}), f32[8,64,128]{2,1,0:T(8,128)S(1)}, u32[]{:S(2)}, u32[]{:S(2)}) async-start(f32[8,64,128]{2,1,0:T(8,128)} %shard_map.84), calls=%async_computation.2 | async-start | bytes 524288 | tf_op jit(solution)/shard_map/all_to_all | solution.py:212
  87.4 12.3 %all-to-all-done.2 = f32[8,64,128]{2,1,0:T(8,128)S(1)} async-done(((f32[8,64,128]{2,1,0:T(8,128)}), f32[8,64,128]{2,1,0:T(8,128)S(1)}, u32[]{:S(2)}, u32[]{:S(2)}) %all-to-all-start.2) | async-done | bytes 262176 | tf_op jit(solution)/shard_map/all_to_all | solution.py:212
  99.7 0.8 fusion
  100.5 14.6 %all_to_all.21 = f32[8,64,128]{2,1,0:T(8,128)S(1)} all-to-all(f32[8,64,128]{2,1,0:T(8,128)S(1)} %broadcast_in_dim.18), channel_id=1, replica_groups=mesh['z'=8,'x'=4,'core'=2,'grp'=8] {'grp'}, dimensions={0} | all-to-all | bytes 524288 | tf_op jit(solution)/shard_map/all_to_all | solution.py:212
  115.2 0.7 copy.14
  (7 shorter events, 0.1 us)
Async XLA Ops:
  0.0 0.7 copy-start
  1.3 14.3 %all-to-all-start = ((s32[8,3,128]{2,1,0:T(4,128)}), s32[8,3,128]{2,1,0:T(4,128)S(1)}, u32[]{:S(2)}, u32[]{:S(2)}) async-start(s32[8,3,128]{2,1,0:T(4,128)} %broadcast_in_dim.16), calls=%async_computation | async-start | bytes 32768 | tf_op jit(solution)/shard_map/all_to_all | solution.py:212
  42.2 13.8 %collective-permute-start = (f32[8,144,128]{2,1,0:T(8,128)S(1)}, f32[8,144,128]{2,1,0:T(8,128)S(1)}, u32[]{:S(2)}, u32[]{:S(2)}) collective-permute-start(f32[8,144,128]{2,1,0:T(8,128)S(1)} %all_to_all.20.refs_0_), channel_id=1, source_target_pairs={{0,16},{16,32},{32,48},{48,0},{1,17},{17,33},{33,49},{49,1},{2,18}... | collective-permute-start | bytes 1769480 | tf_op jit(solution)/shard_map/ppermute | solution.py:204
  45.4 12.6 %collective-permute-start.1 = (f32[8,144,128]{2,1,0:T(8,128)S(1)}, f32[8,144,128]{2,1,0:T(8,128)S(1)}, u32[]{:S(2)}, u32[]{:S(2)}) collective-permute-start(f32[8,144,128]{2,1,0:T(8,128)S(1)} %all_to_all.20.refs_0_), channel_id=1, source_target_pairs={{0,48},{16,0},{32,16},{48,32},{1,49},{17,1},{33,17},{49,33},{2,50}... | collective-permute-start | bytes 1769480 | tf_op jit(solution)/shard_map/ppermute | solution.py:204
  48.7 23.3 %collective-permute-start.4 = (f32[8,144,128]{2,1,0:T(8,128)S(1)}, f32[8,144,128]{2,1,0:T(8,128)S(1)}, u32[]{:S(2)}, u32[]{:S(2)}) collective-permute-start(f32[8,144,128]{2,1,0:T(8,128)S(1)} %all_to_all.20.refs_0_), channel_id=1, source_target_pairs={{0,8},{8,0},{1,9},{9,1},{2,10},{10,2},{3,11},{11,3},{4,12},{12,4},... | collective-permute-start | bytes 1769480 | tf_op jit(solution)/shard_map/ppermute | solution.py:208
  56.0 16.0 %collective-permute-start.2 = (f32[4,144,128]{2,1,0:T(8,128)S(1)}, f32[4,144,128]{2,1,0:T(8,128)S(1)}, u32[]{:S(2)}, u32[]{:S(2)}) collective-permute-start(f32[4,144,128]{2,1,0:T(8,128)S(1)} %slice.8), channel_id=1, source_target_pairs={{0,16},{16,32},{32,48},{48,0},{1,17},{17,33},{33,49},{49,1},{2,18}... | collective-permute-start | bytes 884744 | tf_op jit(solution)/shard_map/ppermute | solution.py:204
  58.0 14.1 %collective-permute-start.3 = (f32[4,144,128]{2,1,0:T(8,128)S(1)}, f32[4,144,128]{2,1,0:T(8,128)S(1)}, u32[]{:S(2)}, u32[]{:S(2)}) collective-permute-start(f32[4,144,128]{2,1,0:T(8,128)S(1)} %slice.9), channel_id=1, source_target_pairs={{0,48},{16,0},{32,16},{48,32},{1,49},{17,1},{33,17},{49,33},{2,50}... | collective-permute-start | bytes 884744 | tf_op jit(solution)/shard_map/ppermute | solution.py:204
  62.6 12.0 %collective-permute-start.5 = (f32[8,144,128]{2,1,0:T(8,128)S(1)}, f32[8,144,128]{2,1,0:T(8,128)S(1)}, u32[]{:S(2)}, u32[]{:S(2)}) collective-permute-start(f32[8,144,128]{2,1,0:T(8,128)S(1)} %collective-permute-done.refs_1_), channel_id=1, source_target_pairs={{0,8},{8,0},{1,9},{9,1},{2,10},{10,2},{3,11},{11,3},{4,12},{12,4},... | collective-permute-start | bytes 1769480 | tf_op jit(solution)/shard_map/ppermute | solution.py:208
  70.1 4.4 %collective-permute-start.6 = (f32[8,144,128]{2,1,0:T(8,128)S(1)}, f32[8,144,128]{2,1,0:T(8,128)S(1)}, u32[]{:S(2)}, u32[]{:S(2)}) collective-permute-start(f32[8,144,128]{2,1,0:T(8,128)S(1)} %collective-permute-done.1.refs_2_), channel_id=1, source_target_pairs={{0,8},{8,0},{1,9},{9,1},{2,10},{10,2},{3,11},{11,3},{4,12},{12,4},... | collective-permute-start | bytes 1769480 | tf_op jit(solution)/shard_map/ppermute | solution.py:208
  72.2 4.0 %collective-permute-start.7 = (f32[8,144,128]{2,1,0:T(8,128)S(1)}, f32[8,144,128]{2,1,0:T(8,128)S(1)}, u32[]{:S(2)}, u32[]{:S(2)}) collective-permute-start(f32[8,144,128]{2,1,0:T(8,128)S(1)} %constant_dynamic-update-slice_fusion.refs_3_), channel_id=1, source_target_pairs={{0,8},{8,0},{1,9},{9,1},{2,10},{10,2},{3,11},{11,3},{4,12},{12,4},... | collective-permute-start | bytes 1769480 | tf_op jit(solution)/shard_map/ppermute | solution.py:208
  84.0 15.7 %all-to-all-start.2 = ((f32[8,64,128]{2,1,0:T(8,128)}), f32[8,64,128]{2,1,0:T(8,128)S(1)}, u32[]{:S(2)}, u32[]{:S(2)}) async-start(f32[8,64,128]{2,1,0:T(8,128)} %shard_map.84), calls=%async_computation.2 | async-start | bytes 524288 | tf_op jit(solution)/shard_map/all_to_all | solution.py:212

commit v7 on v6

--- a/solution.py
+++ b/solution.py
@@ -38,22 +38,19 @@
 
 
 def payload_kernel(counts_ref, tiles_ref, lists_ref, amp_ref, int_ref, res_ref, out_ref, joined):
-    owner = lax.broadcasted_iota(jnp.int32, (OWNERS, TB), 0)
+    owner = lax.broadcasted_iota(jnp.int32, (OWNERS, MEMBERS * TB), 0)
     slot = lax.broadcasted_iota(jnp.int32, (OWNERS, TB), 1)
+    live = jnp.concatenate([(slot < counts_ref[0, m]).astype(jnp.float32) for m in range(MEMBERS)], axis=1)
     number = lax.broadcasted_iota(jnp.int32, (8, OWNERS), 1) * TILES
-
-    def named(m):
-        rows = []
-        for kind, table in enumerate((amp_ref, int_ref, res_ref)):
-            hit = lists_ref[m, kind : kind + 1, :] == owner
-            if kind == 2:
-                hit = hit & (slot < counts_ref[0, m])
-            names = number + table[0:1, :] + (1 if kind == 2 else 0)
-            row = dot(names.astype(jnp.bfloat16), hit.astype(jnp.bfloat16))[0:1]
-            rows.append(row - 1.0 if kind == 2 else row)
-        return jnp.concatenate(rows, axis=0)
-
-    lists = [named(m) for m in range(MEMBERS)]
+    kinds = []
+    for kind, table in enumerate((amp_ref, int_ref, res_ref)):
+        hit = jnp.concatenate([lists_ref[m, kind : kind + 1, :] for m in range(MEMBERS)], axis=1) == owner
+        hit = jnp.where(hit, live if kind == 2 else 1.0, 0.0)
+        names = number + table[0:1, :] + (1 if kind == 2 else 0)
+        row = dot(names.astype(jnp.bfloat16), hit.astype(jnp.bfloat16))[0:1]
+        kinds.append(row - 1.0 if kind == 2 else row)
+    kinds = jnp.concatenate(kinds, axis=0)
+    lists = [kinds[:, m * TB : (m + 1) * TB] for m in range(MEMBERS)]
     joined[...] = jnp.full_like(joined, -1.0)
     lane = lax.broadcasted_iota(jnp.int32, (3, TB), 1)
     at = jnp.int32(0)

time: 117 us -> 117 us (level)
  no operation moved by 1% of the time
where the time goes in v7:
time: 117 us; the launch traced here: 116 us
  starting transfers between devices  42.6 us (36%)
  blocking collectives  40.2 us (34%)
  waiting for transfers between devices  19.9 us (17%)
  Pallas kernels  10.1 us (9%)
  local copies, waits for them, and re-layouts  2.1 us (2%)
    all_to_all x2, blocking collectives, swap(): return lax.all_to_all(block, axis, split_axis=0, concat_axis=0, tiled=True)  40.2 us
    ppermute x4, starting transfers between devices, across(): return lax.ppermute(block, 'core', [(0, 1), (1, 0)])  18.5 us
    all_to_all x2, waiting for transfers between devices, swap(): return lax.all_to_all(block, axis, split_axis=0, concat_axis=0, tiled=True)  17.7 us
    ppermute x4, starting transfers between devices, shift(): return lax.ppermute(block, 'x', [(i, (i + by) % 4) for i in range(4)])  13 us
    all_to_all x2, starting transfers between devices, swap(): return lax.all_to_all(block, axis, split_axis=0, concat_axis=0, tiled=True)  11.1 us
    pallas_call x1, Pallas kernels, local(): pl.pallas_call(ladder_kernel, out_shape=pltpu.VMEM((MEMBERS, TB // 2, TB)...  7.82 us
  transfers between devices with their start and end apart: 10, of which 4 were waited for; matrix products, arithmetic and copies ran while one was open for 0% of the time, Pallas kernels for 1%

profile of v7, /device:TPU:1, one launch (start us, length us, event | category | flops | bytes accessed | tf_op | source)
XLA Modules:
  0.0 115.8 jit_solution(3989701164468368478)
XLA Ops:
  0.0 0.0 copy-start
  0.0 0.7 copy-done
  0.7 0.6 broadcast_in_dim.16
  1.3 7.7 %all-to-all-start = ((s32[8,3,128]{2,1,0:T(4,128)}), s32[8,3,128]{2,1,0:T(4,128)S(1)}, u32[]{:S(2)}, u32[]{:S(2)}) async-start(s32[8,3,128]{2,1,0:T(4,128)} %broadcast_in_dim.16), calls=%async_computation | async-start | bytes 32768 | tf_op jit(solution)/shard_map/all_to_all | solution.py:209
  8.9 1.2 %shard_map.82.tiles_ref = f32[128,128]{1,0:T(8,128)S(1)} custom-call(f32[4,128,128]{2,1,0:T(8,128)} %amp_ref.2, f32[4,128,128]{2,1,0:T(8,128)} %int_ref.2), custom_call_target="tpu_custom_call" | custom-call | tf_op jit(solution)/shard_map/pallas_call | solution.py:216
  10.2 5.4 %all-to-all-done.lists_ref = s32[8,3,128]{2,1,0:T(4,128)S(1)} async-done(((s32[8,3,128]{2,1,0:T(4,128)}), s32[8,3,128]{2,1,0:T(4,128)S(1)}, u32[]{:S(2)}, u32[]{:S(2)}) %all-to-all-start) | async-done | bytes 12320 | tf_op jit(solution)/shard_map/all_to_all | solution.py:209
  15.6 1.1 shard_map.83
  16.7 25.5 %all_to_all.20.refs_0_ = f32[8,144,128]{2,1,0:T(8,128)S(1)} all-to-all(f32[8,144,128]{2,1,0:T(8,128)S(1)} %shard_map.83), channel_id=1, replica_groups=mesh['z'=8,'x'=4,'core'=2,'grp'=8] {'z'}, dimensions={0} | all-to-all | bytes 1179648 | tf_op jit(solution)/shard_map/all_to_all | solution.py:209
  42.2 3.1 %collective-permute-start = (f32[8,144,128]{2,1,0:T(8,128)S(1)}, f32[8,144,128]{2,1,0:T(8,128)S(1)}, u32[]{:S(2)}, u32[]{:S(2)}) collective-permute-start(f32[8,144,128]{2,1,0:T(8,128)S(1)} %all_to_all.20.refs_0_), channel_id=1, source_target_pairs={{0,16},{16,32},{32,48},{48,0},{1,17},{17,33},{33,49},{49,1},{2,18}... | collective-permute-start | bytes 1769480 | tf_op jit(solution)/shard_map/ppermute | solution.py:201
  45.3 3.4 %collective-permute-start.1 = (f32[8,144,128]{2,1,0:T(8,128)S(1)}, f32[8,144,128]{2,1,0:T(8,128)S(1)}, u32[]{:S(2)}, u32[]{:S(2)}) collective-permute-start(f32[8,144,128]{2,1,0:T(8,128)S(1)} %all_to_all.20.refs_0_), channel_id=1, source_target_pairs={{0,48},{16,0},{32,16},{48,32},{1,49},{17,1},{33,17},{49,33},{2,50}... | collective-permute-start | bytes 1769480 | tf_op jit(solution)/shard_map/ppermute | solution.py:201
  48.7 6.6 %collective-permute-start.4 = (f32[8,144,128]{2,1,0:T(8,128)S(1)}, f32[8,144,128]{2,1,0:T(8,128)S(1)}, u32[]{:S(2)}, u32[]{:S(2)}) collective-permute-start(f32[8,144,128]{2,1,0:T(8,128)S(1)} %all_to_all.20.refs_0_), channel_id=1, source_target_pairs={{0,8},{8,0},{1,9},{9,1},{2,10},{10,2},{3,11},{11,3},{4,12},{12,4},... | collective-permute-start | bytes 1769480 | tf_op jit(solution)/shard_map/ppermute | solution.py:205
  55.3 0.6 collective-permute-done.refs_1_
  56.0 1.9 %collective-permute-start.2 = (f32[4,144,128]{2,1,0:T(8,128)S(1)}, f32[4,144,128]{2,1,0:T(8,128)S(1)}, u32[]{:S(2)}, u32[]{:S(2)}) collective-permute-start(f32[4,144,128]{2,1,0:T(8,128)S(1)} %slice.8), channel_id=1, source_target_pairs={{0,16},{16,32},{32,48},{48,0},{1,17},{17,33},{33,49},{49,1},{2,18}... | collective-permute-start | bytes 884744 | tf_op jit(solution)/shard_map/ppermute | solution.py:201
  57.9 0.0 collective-permute-done.1.refs_2_
  57.9 4.6 %collective-permute-start.3 = (f32[4,144,128]{2,1,0:T(8,128)S(1)}, f32[4,144,128]{2,1,0:T(8,128)S(1)}, u32[]{:S(2)}, u32[]{:S(2)}) collective-permute-start(f32[4,144,128]{2,1,0:T(8,128)S(1)} %slice.9), channel_id=1, source_target_pairs={{0,48},{16,0},{32,16},{48,32},{1,49},{17,1},{33,17},{49,33},{2,50}... | collective-permute-start | bytes 884744 | tf_op jit(solution)/shard_map/ppermute | solution.py:201
  62.5 7.5 %collective-permute-start.5 = (f32[8,144,128]{2,1,0:T(8,128)S(1)}, f32[8,144,128]{2,1,0:T(8,128)S(1)}, u32[]{:S(2)}, u32[]{:S(2)}) collective-permute-start(f32[8,144,128]{2,1,0:T(8,128)S(1)} %collective-permute-done.refs_1_), channel_id=1, source_target_pairs={{0,8},{8,0},{1,9},{9,1},{2,10},{10,2},{3,11},{11,3},{4,12},{12,4},... | collective-permute-start | bytes 1769480 | tf_op jit(solution)/shard_map/ppermute | solution.py:205
  70.1 1.9 %collective-permute-start.6 = (f32[8,144,128]{2,1,0:T(8,128)S(1)}, f32[8,144,128]{2,1,0:T(8,128)S(1)}, u32[]{:S(2)}, u32[]{:S(2)}) collective-permute-start(f32[8,144,128]{2,1,0:T(8,128)S(1)} %collective-permute-done.1.refs_2_), channel_id=1, source_target_pairs={{0,8},{8,0},{1,9},{9,1},{2,10},{10,2},{3,11},{11,3},{4,12},{12,4},... | collective-permute-start | bytes 1769480 | tf_op jit(solution)/shard_map/ppermute | solution.py:205
  72.0 0.0 collective-permute-done.4.refs_4_
  72.0 0.0 collective-permute-done.2
  72.0 0.0 collective-permute-done.3
  72.1 2.4 %collective-permute-start.7 = (f32[8,144,128]{2,1,0:T(8,128)S(1)}, f32[8,144,128]{2,1,0:T(8,128)S(1)}, u32[]{:S(2)}, u32[]{:S(2)}) collective-permute-start(f32[8,144,128]{2,1,0:T(8,128)S(1)} %constant_dynamic-update-slice_fusion.refs_3_), channel_id=1, source_target_pairs={{0,8},{8,0},{1,9},{9,1},{2,10},{10,2},{3,11},{11,3},{4,12},{12,4},... | collective-permute-start | bytes 1769480 | tf_op jit(solution)/shard_map/ppermute | solution.py:205
  74.5 0.0 collective-permute-done.5.refs_5_
  74.5 0.0 collective-permute-done.6.refs_6_
  74.5 1.6 %collective-permute-done.7.refs_7_ = f32[8,144,128]{2,1,0:T(8,128)S(1)} collective-permute-done((f32[8,144,128]{2,1,0:T(8,128)S(1)}, f32[8,144,128]{2,1,0:T(8,128)S(1)}, u32[]{:S(2)}, u32[]{:S(2)}) %collective-permute-start.7) | collective-permute-done | bytes 589856 | tf_op jit(solution)/shard_map/ppermute | solution.py:205
  76.1 7.8 %shard_map.84 = f32[8,64,128]{2,1,0:T(8,128)} custom-call(f32[8,144,128]{2,1,0:T(8,128)S(1)} %all_to_all.20.refs_0_, f32[8,144,128]{2,1,0:T(8,128)S(1)} %collective-permute-done.refs_1_, f32[8,144,128]{2,1,0:T(8,128)S(1)} %collective-permute-done.1.refs_2_, f32[8,144,128]{2,1,0:T(8,128)S(1)} %constant_dynamic-update-slice_fusion.refs_3_, ...), custom_call_target="tpu_custom_call" | custom-call | tf_op jit(solution)/shard_map/pallas_call | solution.py:237
  83.9 3.4 %all-to-all-start.2 = ((f32[8,64,128]{2,1,0:T(8,128)}), f32[8,64,128]{2,1,0:T(8,128)S(1)}, u32[]{:S(2)}, u32[]{:S(2)}) async-start(f32[8,64,128]{2,1,0:T(8,128)} %shard_map.84), calls=%async_computation.2 | async-start | bytes 524288 | tf_op jit(solution)/shard_map/all_to_all | solution.py:209
  87.4 12.3 %all-to-all-done.2 = f32[8,64,128]{2,1,0:T(8,128)S(1)} async-done(((f32[8,64,128]{2,1,0:T(8,128)}), f32[8,64,128]{2,1,0:T(8,128)S(1)}, u32[]{:S(2)}, u32[]{:S(2)}) %all-to-all-start.2) | async-done | bytes 262176 | tf_op jit(solution)/shard_map/all_to_all | solution.py:209
  99.7 0.8 fusion
  100.5 14.6 %all_to_all.21 = f32[8,64,128]{2,1,0:T(8,128)S(1)} all-to-all(f32[8,64,128]{2,1,0:T(8,128)S(1)} %broadcast_in_dim.18), channel_id=1, replica_groups=mesh['z'=8,'x'=4,'core'=2,'grp'=8] {'grp'}, dimensions={0} | all-to-all | bytes 524288 | tf_op jit(solution)/shard_map/all_to_all | solution.py:209
  115.1 0.7 copy.14
  (7 shorter events, 0.1 us)
Async XLA Ops:
  0.0 0.7 copy-start
  1.3 14.3 %all-to-all-start = ((s32[8,3,128]{2,1,0:T(4,128)}), s32[8,3,128]{2,1,0:T(4,128)S(1)}, u32[]{:S(2)}, u32[]{:S(2)}) async-start(s32[8,3,128]{2,1,0:T(4,128)} %broadcast_in_dim.16), calls=%async_computation | async-start | bytes 32768 | tf_op jit(solution)/shard_map/all_to_all | solution.py:209
  42.2 13.8 %collective-permute-start = (f32[8,144,128]{2,1,0:T(8,128)S(1)}, f32[8,144,128]{2,1,0:T(8,128)S(1)}, u32[]{:S(2)}, u32[]{:S(2)}) collective-permute-start(f32[8,144,128]{2,1,0:T(8,128)S(1)} %all_to_all.20.refs_0_), channel_id=1, source_target_pairs={{0,16},{16,32},{32,48},{48,0},{1,17},{17,33},{33,49},{49,1},{2,18}... | collective-permute-start | bytes 1769480 | tf_op jit(solution)/shard_map/ppermute | solution.py:201
  45.3 12.6 %collective-permute-start.1 = (f32[8,144,128]{2,1,0:T(8,128)S(1)}, f32[8,144,128]{2,1,0:T(8,128)S(1)}, u32[]{:S(2)}, u32[]{:S(2)}) collective-permute-start(f32[8,144,128]{2,1,0:T(8,128)S(1)} %all_to_all.20.refs_0_), channel_id=1, source_target_pairs={{0,48},{16,0},{32,16},{48,32},{1,49},{17,1},{33,17},{49,33},{2,50}... | collective-permute-start | bytes 1769480 | tf_op jit(solution)/shard_map/ppermute | solution.py:201
  48.7 23.3 %collective-permute-start.4 = (f32[8,144,128]{2,1,0:T(8,128)S(1)}, f32[8,144,128]{2,1,0:T(8,128)S(1)}, u32[]{:S(2)}, u32[]{:S(2)}) collective-permute-start(f32[8,144,128]{2,1,0:T(8,128)S(1)} %all_to_all.20.refs_0_), channel_id=1, source_target_pairs={{0,8},{8,0},{1,9},{9,1},{2,10},{10,2},{3,11},{11,3},{4,12},{12,4},... | collective-permute-start | bytes 1769480 | tf_op jit(solution)/shard_map/ppermute | solution.py:205
  56.0 16.0 %collective-permute-start.2 = (f32[4,144,128]{2,1,0:T(8,128)S(1)}, f32[4,144,128]{2,1,0:T(8,128)S(1)}, u32[]{:S(2)}, u32[]{:S(2)}) collective-permute-start(f32[4,144,128]{2,1,0:T(8,128)S(1)} %slice.8), channel_id=1, source_target_pairs={{0,16},{16,32},{32,48},{48,0},{1,17},{17,33},{33,49},{49,1},{2,18}... | collective-permute-start | bytes 884744 | tf_op jit(solution)/shard_map/ppermute | solution.py:201
  57.9 14.1 %collective-permute-start.3 = (f32[4,144,128]{2,1,0:T(8,128)S(1)}, f32[4,144,128]{2,1,0:T(8,128)S(1)}, u32[]{:S(2)}, u32[]{:S(2)}) collective-permute-start(f32[4,144,128]{2,1,0:T(8,128)S(1)} %slice.9), channel_id=1, source_target_pairs={{0,48},{16,0},{32,16},{48,32},{1,49},{17,1},{33,17},{49,33},{2,50}... | collective-permute-start | bytes 884744 | tf_op jit(solution)/shard_map/ppermute | solution.py:201
  62.5 12.0 %collective-permute-start.5 = (f32[8,144,128]{2,1,0:T(8,128)S(1)}, f32[8,144,128]{2,1,0:T(8,128)S(1)}, u32[]{:S(2)}, u32[]{:S(2)}) collective-permute-start(f32[8,144,128]{2,1,0:T(8,128)S(1)} %collective-permute-done.refs_1_), channel_id=1, source_target_pairs={{0,8},{8,0},{1,9},{9,1},{2,10},{10,2},{3,11},{11,3},{4,12},{12,4},... | collective-permute-start | bytes 1769480 | tf_op jit(solution)/shard_map/ppermute | solution.py:205
  70.1 4.4 %collective-permute-start.6 = (f32[8,144,128]{2,1,0:T(8,128)S(1)}, f32[8,144,128]{2,1,0:T(8,128)S(1)}, u32[]{:S(2)}, u32[]{:S(2)}) collective-permute-start(f32[8,144,128]{2,1,0:T(8,128)S(1)} %collective-permute-done.1.refs_2_), channel_id=1, source_target_pairs={{0,8},{8,0},{1,9},{9,1},{2,10},{10,2},{3,11},{11,3},{4,12},{12,4},... | collective-permute-start | bytes 1769480 | tf_op jit(solution)/shard_map/ppermute | solution.py:205
  72.1 4.0 %collective-permute-start.7 = (f32[8,144,128]{2,1,0:T(8,128)S(1)}, f32[8,144,128]{2,1,0:T(8,128)S(1)}, u32[]{:S(2)}, u32[]{:S(2)}) collective-permute-start(f32[8,144,128]{2,1,0:T(8,128)S(1)} %constant_dynamic-update-slice_fusion.refs_3_), channel_id=1, source_target_pairs={{0,8},{8,0},{1,9},{9,1},{2,10},{10,2},{3,11},{11,3},{4,12},{12,4},... | collective-permute-start | bytes 1769480 | tf_op jit(solution)/shard_map/ppermute | solution.py:205
  83.9 15.7 %all-to-all-start.2 = ((f32[8,64,128]{2,1,0:T(8,128)}), f32[8,64,128]{2,1,0:T(8,128)S(1)}, u32[]{:S(2)}, u32[]{:S(2)}) async-start(f32[8,64,128]{2,1,0:T(8,128)} %shard_map.84), calls=%async_computation.2 | async-start | bytes 524288 | tf_op jit(solution)/shard_map/all_to_all | solution.py:209
